TPU v7x, 256 devices: a whole 4x4x8 slice. The times are simulated.
256 devices in a mesh: turn: 32 (over z_hi, x, core), line: 8 (over z_lo, y).
Axes of the slice: x: 4, y: 4, z: 8 (z_hi: 4, z_lo: 2; z = z_hi * 2 + z_lo), core: 2. Of those that a mesh axis runs over, the one named last changes fastest.
Arguments:
- flop_cards: int32 [2, 3], replicated, may hold values from 0 to 51, as said below
- turn_cards: int32 [2, 32], P(None, 'turn'), may hold values from 0 to 51, as said below
- river_cards: int32 [2, 32, 8], P(None, 'turn'), may hold values from 0 to 51, as said below
- ranks: int32 [2, 32, 8, 1326], P(None, 'turn'), may hold values from 0 to 7461
- flop_reach: float32 [2, 1326], replicated, may hold values from 0.05 to 1
- turn_policy: bfloat16 [2, 32, 8, 4, 1326], P(None, 'turn', 'line'), may hold values from 0.049804688 to 1
- river_policy: bfloat16 [2, 32, 8, 8, 4, 4, 4, 1326], P(None, 'turn', None, 'line'), may hold values from 0.049804688 to 1
- stake: float32 [8, 4, 4, 4], P('line'), may hold values from 0.5 to 4
Outputs:
- turn_values: float32 [2, 32, 1326], P(None, 'turn')
- flop_value: float32 [2, 1326], replicated
Inputs may be any that keep to these rules, and one draw needn't show every extreme that they name: `turn_cards`: for each flop, the flop cards and the turn cards are distinct cards of 0 to 51. `river_cards`: under each turn card the river cards are distinct and differ from that turn card and the flop cards. `flop_cards`: distinct from the turn and river cards of the same flop; the first flop holds card 52 - 1.
All inputs are finite; a program needn't handle non-finite values.
Results may differ from a plain program's by a relative error of at most 0.0003.
Values may be sent and summed in bfloat16 or wider, within the bound.
No kernel may reach another device: no remote copies, remote signals or barrier semaphores. Data moves between devices by JAX's collectives and lax.ppermute only.
A program may use at most 64 MiB of HBM per device.

v0:
```python
import jax
import jax.numpy as jnp
import numpy as np
from jax import lax
from jax.sharding import PartitionSpec as P

CARDS = 52


def hand_cards():
    lower_card, upper_card = np.triu_indices(CARDS, 1)
    return (jnp.asarray(lower_card.astype(np.int32)), jnp.asarray(upper_card.astype(np.int32)))


def unblocked_by(cards, lower_card, upper_card):
    column = cards[..., :, None]
    struck = (lower_card == column) | (upper_card == column)
    return 1.0 - jnp.any(struck, axis=-2).astype(jnp.float32)


def card_conflict(lower_card, upper_card):
    return (
        (lower_card[:, None] == lower_card[None, :])
        | (lower_card[:, None] == upper_card[None, :])
        | (upper_card[:, None] == lower_card[None, :])
        | (upper_card[:, None] == upper_card[None, :])
    )


def showdown(strength, line_reach, shared_card):
    verdict = jnp.sign(strength[None, :] - strength[:, None]).astype(jnp.float32)
    payoff = jnp.where(shared_card, 0.0, verdict).astype(jnp.bfloat16)
    return jnp.dot(line_reach, payoff, preferred_element_type=jnp.float32)


def board_values(reach, strengths, unblocked, pots, shared_card):
    flops, boards = (reach.shape[0], reach.shape[1])
    hand_count = reach.shape[-1]

    def one_board(position):
        flop_index = position // boards
        board_index = position % boards
        line_reach = reach[flop_index, board_index].reshape(-1, hand_count)
        leaves = showdown(strengths[flop_index, board_index], line_reach, shared_card)
        leaves = leaves.reshape(reach.shape[2:]) * pots[..., None]
        values = jnp.max(jnp.sum(leaves, axis=3), axis=2)
        return jnp.sum(values, axis=1) * unblocked[flop_index, board_index][None, :]

    totals = lax.map(one_board, jnp.arange(flops * boards, dtype=jnp.int32))
    return jnp.sum(totals.reshape(flops, boards, reach.shape[2], hand_count), axis=1)


def local(flop_cards, turn_cards, river_cards, ranks, flop_reach, turn_policy, river_policy, stake):
    lower_card, upper_card = hand_cards()
    shared_card = card_conflict(lower_card, upper_card)
    rivers = river_cards.shape[2]
    flop_clear = unblocked_by(flop_cards, lower_card, upper_card)
    turn_clear = flop_clear * unblocked_by(turn_cards, lower_card, upper_card)
    unblocked = turn_clear[:, None, :] * unblocked_by(
        river_cards[:, 0, :, None], lower_card, upper_card
    )
    opening = flop_reach * flop_clear
    turn_weights = turn_policy[:, 0].astype(jnp.float32)
    turn_prob = turn_weights / jnp.sum(turn_weights, axis=2, keepdims=True)
    river_weights = river_policy[:, 0].astype(jnp.float32)
    river_prob = river_weights / jnp.sum(river_weights, axis=5, keepdims=True)
    reach = (
        (opening[:, None, :] * unblocked)[:, :, None, None, None, None, :]
        * turn_prob[:, None, :, :, None, None, :]
        * river_prob
    )
    reach = reach.astype(jnp.bfloat16)
    strengths = ranks[:, 0]
    totals = board_values(reach, strengths, unblocked, stake, shared_card) / rivers
    turn_values = lax.pmax(totals, "line")
    turn_total = turn_values.shape[1] * lax.axis_size("turn")
    flop_value = lax.psum(jnp.sum(turn_values, axis=1), "turn") / turn_total
    return (turn_values, flop_value)


def solution(mesh):
    in_specs = (
        P(),
        P(None, "turn"),
        P(None, "turn", None),
        P(None, "turn", None, None),
        P(),
        P(None, "turn", "line", None, None),
        P(None, "turn", None, "line", None, None, None, None),
        P("line", None, None, None),
    )
    out_specs = (P(None, "turn", None), P())
    return jax.shard_map(local, mesh=mesh, in_specs=in_specs, out_specs=out_specs, check_vma=False)
```

profile of v0, /device:TPU:32, one launch (start us, length us, event | category | flops | bytes accessed | tf_op | source)
XLA Modules:
  0.0 333.6 jit_solution(15805887972155032975)
XLA Ops:
  0.6 1.0 or_reduce_fusion
  1.6 0.8 fusion.22
  2.5 0.8 subtract_multiply_fusion
  3.3 0.8 convert_reduce_fusion.1
  4.1 0.8 fusion.20
  4.9 5.9 %convert_reduce_fusion = f32[2,8,4,4,1326]{4,3,2,1,0:T(4,128)S(1)} fusion(bf16[2,1,8,1,4,4,4,1326]{7,6,5,4,3,2,1,0:T(4,128)(2,1)} %param.18), kind=kLoop, calls=%fused_computation.14 | loop fusion | flops 2376192 | bytes 4073472 | tf_op jit(solution)/shard_map/reduce_sum | solution.py:66
  10.9 2.4 fusion.19
  13.3 145.7 %while.13 = (s32[]{:T(128)}, f32[16,1,1326]{2,0,1:T(8,128)S(1)}, s32[16]{0:T(128)S(1)}, bf16[2,8,1,4,4,4,1326]{6,5,4,3,2,1,0:T(4,128)(2,1)S(1)}, s32[2,8,1326]{2...) while((s32[]{:T(128)}, f32[16,1,1326]{2,0,1:T(8,128)S(1)}, ...), condition=%wide.region_7.8_spmd.clone, body=%wide.region_3.7_spmd.clone.sunk | while | flops 246328416 | bytes 492628 | solution.py:49
  13.4 0.6 dynamic_slice.42
  16.6 0.8 dynamic-slice_reduce_fusion.2
  17.4 4.8 %fusion.29 = f32[4,4,1326]{2,1,0:T(4,128)S(1)} fusion(s32[1326]{0:T(1024)S(1)} %get-tuple-element.250, s32[1326]{0:T(1024)S(1)} %get-tuple-element.249, s32[1326]{0:T(1024)S(1)} %dynamic-slice_reduce_fusion.2, f32[4,4,4]{2,1,0:T(4,128)S(1)} %bitcast.53, bf16[2,8,1,4,4,4,1326]{6,5,4,3,2,1,0:T(4,128)(2,1)S(1)} %get-tuple-element.245, ...), kind=kOutput, calls=%fused_computation.7.clone.1 | convolution fusion | flops 246307152 | bytes 322440 | tf_op jit(solution)/shard_map/while/body/eval_jaxpr/dot_general | solution.py:33
  22.3 0.1 dynamic_update_slice.9
  22.5 0.6 dynamic_slice.42
  25.7 0.8 dynamic-slice_reduce_fusion.2
  26.5 4.8 %fusion.29 = f32[4,4,1326]{2,1,0:T(4,128)S(1)} fusion(s32[1326]{0:T(1024)S(1)} %get-tuple-element.250, s32[1326]{0:T(1024)S(1)} %get-tuple-element.249, s32[1326]{0:T(1024)S(1)} %dynamic-slice_reduce_fusion.2, f32[4,4,4]{2,1,0:T(4,128)S(1)} %bitcast.53, bf16[2,8,1,4,4,4,1326]{6,5,4,3,2,1,0:T(4,128)(2,1)S(1)} %get-tuple-element.245, ...), kind=kOutput, calls=%fused_computation.7.clone.1 | convolution fusion | flops 246307152 | bytes 322440 | tf_op jit(solution)/shard_map/while/body/eval_jaxpr/dot_general | solution.py:33
  31.4 0.1 dynamic_update_slice.9
  31.6 0.6 dynamic_slice.42
  34.8 0.8 dynamic-slice_reduce_fusion.2
  35.6 4.8 %fusion.29 = f32[4,4,1326]{2,1,0:T(4,128)S(1)} fusion(s32[1326]{0:T(1024)S(1)} %get-tuple-element.250, s32[1326]{0:T(1024)S(1)} %get-tuple-element.249, s32[1326]{0:T(1024)S(1)} %dynamic-slice_reduce_fusion.2, f32[4,4,4]{2,1,0:T(4,128)S(1)} %bitcast.53, bf16[2,8,1,4,4,4,1326]{6,5,4,3,2,1,0:T(4,128)(2,1)S(1)} %get-tuple-element.245, ...), kind=kOutput, calls=%fused_computation.7.clone.1 | convolution fusion | flops 246307152 | bytes 322440 | tf_op jit(solution)/shard_map/while/body/eval_jaxpr/dot_general | solution.py:33
  40.7 0.6 dynamic_slice.42
  43.9 0.8 dynamic-slice_reduce_fusion.2
  44.7 4.8 %fusion.29 = f32[4,4,1326]{2,1,0:T(4,128)S(1)} fusion(s32[1326]{0:T(1024)S(1)} %get-tuple-element.250, s32[1326]{0:T(1024)S(1)} %get-tuple-element.249, s32[1326]{0:T(1024)S(1)} %dynamic-slice_reduce_fusion.2, f32[4,4,4]{2,1,0:T(4,128)S(1)} %bitcast.53, bf16[2,8,1,4,4,4,1326]{6,5,4,3,2,1,0:T(4,128)(2,1)S(1)} %get-tuple-element.245, ...), kind=kOutput, calls=%fused_computation.7.clone.1 | convolution fusion | flops 246307152 | bytes 322440 | tf_op jit(solution)/shard_map/while/body/eval_jaxpr/dot_general | solution.py:33
  49.6 0.1 dynamic_update_slice.9
  49.8 0.6 dynamic_slice.42
  53.0 0.8 dynamic-slice_reduce_fusion.2
  53.8 4.8 %fusion.29 = f32[4,4,1326]{2,1,0:T(4,128)S(1)} fusion(s32[1326]{0:T(1024)S(1)} %get-tuple-element.250, s32[1326]{0:T(1024)S(1)} %get-tuple-element.249, s32[1326]{0:T(1024)S(1)} %dynamic-slice_reduce_fusion.2, f32[4,4,4]{2,1,0:T(4,128)S(1)} %bitcast.53, bf16[2,8,1,4,4,4,1326]{6,5,4,3,2,1,0:T(4,128)(2,1)S(1)} %get-tuple-element.245, ...), kind=kOutput, calls=%fused_computation.7.clone.1 | convolution fusion | flops 246307152 | bytes 322440 | tf_op jit(solution)/shard_map/while/body/eval_jaxpr/dot_general | solution.py:33
  58.7 0.1 dynamic_update_slice.9
  58.9 0.6 dynamic_slice.42
  62.1 0.8 dynamic-slice_reduce_fusion.2
  62.9 4.8 %fusion.29 = f32[4,4,1326]{2,1,0:T(4,128)S(1)} fusion(s32[1326]{0:T(1024)S(1)} %get-tuple-element.250, s32[1326]{0:T(1024)S(1)} %get-tuple-element.249, s32[1326]{0:T(1024)S(1)} %dynamic-slice_reduce_fusion.2, f32[4,4,4]{2,1,0:T(4,128)S(1)} %bitcast.53, bf16[2,8,1,4,4,4,1326]{6,5,4,3,2,1,0:T(4,128)(2,1)S(1)} %get-tuple-element.245, ...), kind=kOutput, calls=%fused_computation.7.clone.1 | convolution fusion | flops 246307152 | bytes 322440 | tf_op jit(solution)/shard_map/while/body/eval_jaxpr/dot_general | solution.py:33
  67.8 0.1 dynamic_update_slice.9
  68.0 0.6 dynamic_slice.42
  71.2 0.8 dynamic-slice_reduce_fusion.2
  72.0 4.8 %fusion.29 = f32[4,4,1326]{2,1,0:T(4,128)S(1)} fusion(s32[1326]{0:T(1024)S(1)} %get-tuple-element.250, s32[1326]{0:T(1024)S(1)} %get-tuple-element.249, s32[1326]{0:T(1024)S(1)} %dynamic-slice_reduce_fusion.2, f32[4,4,4]{2,1,0:T(4,128)S(1)} %bitcast.53, bf16[2,8,1,4,4,4,1326]{6,5,4,3,2,1,0:T(4,128)(2,1)S(1)} %get-tuple-element.245, ...), kind=kOutput, calls=%fused_computation.7.clone.1 | convolution fusion | flops 246307152 | bytes 322440 | tf_op jit(solution)/shard_map/while/body/eval_jaxpr/dot_general | solution.py:33
  77.1 0.6 dynamic_slice.42
  80.3 0.8 dynamic-slice_reduce_fusion.2
  81.1 4.8 %fusion.29 = f32[4,4,1326]{2,1,0:T(4,128)S(1)} fusion(s32[1326]{0:T(1024)S(1)} %get-tuple-element.250, s32[1326]{0:T(1024)S(1)} %get-tuple-element.249, s32[1326]{0:T(1024)S(1)} %dynamic-slice_reduce_fusion.2, f32[4,4,4]{2,1,0:T(4,128)S(1)} %bitcast.53, bf16[2,8,1,4,4,4,1326]{6,5,4,3,2,1,0:T(4,128)(2,1)S(1)} %get-tuple-element.245, ...), kind=kOutput, calls=%fused_computation.7.clone.1 | convolution fusion | flops 246307152 | bytes 322440 | tf_op jit(solution)/shard_map/while/body/eval_jaxpr/dot_general | solution.py:33
  86.2 0.6 dynamic_slice.42
  89.4 0.8 dynamic-slice_reduce_fusion.2
  90.2 4.8 %fusion.29 = f32[4,4,1326]{2,1,0:T(4,128)S(1)} fusion(s32[1326]{0:T(1024)S(1)} %get-tuple-element.250, s32[1326]{0:T(1024)S(1)} %get-tuple-element.249, s32[1326]{0:T(1024)S(1)} %dynamic-slice_reduce_fusion.2, f32[4,4,4]{2,1,0:T(4,128)S(1)} %bitcast.53, bf16[2,8,1,4,4,4,1326]{6,5,4,3,2,1,0:T(4,128)(2,1)S(1)} %get-tuple-element.245, ...), kind=kOutput, calls=%fused_computation.7.clone.1 | convolution fusion | flops 246307152 | bytes 322440 | tf_op jit(solution)/shard_map/while/body/eval_jaxpr/dot_general | solution.py:33
  95.3 0.6 dynamic_slice.42
  98.5 0.8 dynamic-slice_reduce_fusion.2
  99.4 4.8 %fusion.29 = f32[4,4,1326]{2,1,0:T(4,128)S(1)} fusion(s32[1326]{0:T(1024)S(1)} %get-tuple-element.250, s32[1326]{0:T(1024)S(1)} %get-tuple-element.249, s32[1326]{0:T(1024)S(1)} %dynamic-slice_reduce_fusion.2, f32[4,4,4]{2,1,0:T(4,128)S(1)} %bitcast.53, bf16[2,8,1,4,4,4,1326]{6,5,4,3,2,1,0:T(4,128)(2,1)S(1)} %get-tuple-element.245, ...), kind=kOutput, calls=%fused_computation.7.clone.1 | convolution fusion | flops 246307152 | bytes 322440 | tf_op jit(solution)/shard_map/while/body/eval_jaxpr/dot_general | solution.py:33
  104.4 0.6 dynamic_slice.42
  107.6 0.8 dynamic-slice_reduce_fusion.2
  108.5 4.8 %fusion.29 = f32[4,4,1326]{2,1,0:T(4,128)S(1)} fusion(s32[1326]{0:T(1024)S(1)} %get-tuple-element.250, s32[1326]{0:T(1024)S(1)} %get-tuple-element.249, s32[1326]{0:T(1024)S(1)} %dynamic-slice_reduce_fusion.2, f32[4,4,4]{2,1,0:T(4,128)S(1)} %bitcast.53, bf16[2,8,1,4,4,4,1326]{6,5,4,3,2,1,0:T(4,128)(2,1)S(1)} %get-tuple-element.245, ...), kind=kOutput, calls=%fused_computation.7.clone.1 | convolution fusion | flops 246307152 | bytes 322440 | tf_op jit(solution)/shard_map/while/body/eval_jaxpr/dot_general | solution.py:33
  113.5 0.6 dynamic_slice.42
  116.7 0.8 dynamic-slice_reduce_fusion.2
  117.6 4.8 %fusion.29 = f32[4,4,1326]{2,1,0:T(4,128)S(1)} fusion(s32[1326]{0:T(1024)S(1)} %get-tuple-element.250, s32[1326]{0:T(1024)S(1)} %get-tuple-element.249, s32[1326]{0:T(1024)S(1)} %dynamic-slice_reduce_fusion.2, f32[4,4,4]{2,1,0:T(4,128)S(1)} %bitcast.53, bf16[2,8,1,4,4,4,1326]{6,5,4,3,2,1,0:T(4,128)(2,1)S(1)} %get-tuple-element.245, ...), kind=kOutput, calls=%fused_computation.7.clone.1 | convolution fusion | flops 246307152 | bytes 322440 | tf_op jit(solution)/shard_map/while/body/eval_jaxpr/dot_general | solution.py:33
  122.6 0.6 dynamic_slice.42
  125.9 0.8 dynamic-slice_reduce_fusion.2
  126.7 4.8 %fusion.29 = f32[4,4,1326]{2,1,0:T(4,128)S(1)} fusion(s32[1326]{0:T(1024)S(1)} %get-tuple-element.250, s32[1326]{0:T(1024)S(1)} %get-tuple-element.249, s32[1326]{0:T(1024)S(1)} %dynamic-slice_reduce_fusion.2, f32[4,4,4]{2,1,0:T(4,128)S(1)} %bitcast.53, bf16[2,8,1,4,4,4,1326]{6,5,4,3,2,1,0:T(4,128)(2,1)S(1)} %get-tuple-element.245, ...), kind=kOutput, calls=%fused_computation.7.clone.1 | convolution fusion | flops 246307152 | bytes 322440 | tf_op jit(solution)/shard_map/while/body/eval_jaxpr/dot_general | solution.py:33
  131.8 0.6 dynamic_slice.42
  135.0 0.8 dynamic-slice_reduce_fusion.2
  135.8 4.8 %fusion.29 = f32[4,4,1326]{2,1,0:T(4,128)S(1)} fusion(s32[1326]{0:T(1024)S(1)} %get-tuple-element.250, s32[1326]{0:T(1024)S(1)} %get-tuple-element.249, s32[1326]{0:T(1024)S(1)} %dynamic-slice_reduce_fusion.2, f32[4,4,4]{2,1,0:T(4,128)S(1)} %bitcast.53, bf16[2,8,1,4,4,4,1326]{6,5,4,3,2,1,0:T(4,128)(2,1)S(1)} %get-tuple-element.245, ...), kind=kOutput, calls=%fused_computation.7.clone.1 | convolution fusion | flops 246307152 | bytes 322440 | tf_op jit(solution)/shard_map/while/body/eval_jaxpr/dot_general | solution.py:33
  140.9 0.6 dynamic_slice.42
  144.1 0.8 dynamic-slice_reduce_fusion.2
  144.9 4.8 %fusion.29 = f32[4,4,1326]{2,1,0:T(4,128)S(1)} fusion(s32[1326]{0:T(1024)S(1)} %get-tuple-element.250, s32[1326]{0:T(1024)S(1)} %get-tuple-element.249, s32[1326]{0:T(1024)S(1)} %dynamic-slice_reduce_fusion.2, f32[4,4,4]{2,1,0:T(4,128)S(1)} %bitcast.53, bf16[2,8,1,4,4,4,1326]{6,5,4,3,2,1,0:T(4,128)(2,1)S(1)} %get-tuple-element.245, ...), kind=kOutput, calls=%fused_computation.7.clone.1 | convolution fusion | flops 246307152 | bytes 322440 | tf_op jit(solution)/shard_map/while/body/eval_jaxpr/dot_general | solution.py:33
  150.0 0.6 dynamic_slice.42
  153.2 0.8 dynamic-slice_reduce_fusion.2
  154.0 4.8 %fusion.29 = f32[4,4,1326]{2,1,0:T(4,128)S(1)} fusion(s32[1326]{0:T(1024)S(1)} %get-tuple-element.250, s32[1326]{0:T(1024)S(1)} %get-tuple-element.249, s32[1326]{0:T(1024)S(1)} %dynamic-slice_reduce_fusion.2, f32[4,4,4]{2,1,0:T(4,128)S(1)} %bitcast.53, bf16[2,8,1,4,4,4,1326]{6,5,4,3,2,1,0:T(4,128)(2,1)S(1)} %get-tuple-element.245, ...), kind=kOutput, calls=%fused_computation.7.clone.1 | convolution fusion | flops 246307152 | bytes 322440 | tf_op jit(solution)/shard_map/while/body/eval_jaxpr/dot_general | solution.py:33
  159.1 33.1 %pmax.7 = f32[2,1,1326]{2,1,0:T(1,128)S(1)} all-reduce(f32[2,1,1326]{2,1,0:T(1,128)S(1)} %div.58), channel_id=1, replica_groups=mesh['turn'=32,'line'=8] {'line'}, use_global_device_ids=true, to_apply=%region_9.10 | all-reduce | flops 2652 | bytes 21216 | tf_op jit(solution)/shard_map/pmax | solution.py:75
  192.2 140.8 %psum.7 = f32[2,1326]{1,0:T(2,128)S(1)} all-reduce(f32[2,1326]{1,0:T(2,128)S(1)} %bitcast.49), channel_id=1, replica_groups=mesh['turn'=32,'line'=8] {'turn'}, use_global_device_ids=true, to_apply=%region_10.11 | all-reduce | flops 2652 | bytes 21216 | tf_op jit(solution)/shard_map/psum | solution.py:77
  333.0 0.6 broadcast_multiply_fusion.2
  (76 shorter events, 3.5 us)
Async XLA Ops:
  0.6 10.2 %copy-start = (bf16[2,1,8,1,4,4,4,1326]{7,6,5,4,3,2,1,0:T(4,128)(2,1)S(1)}, bf16[2,1,8,1,4,4,4,1326]{7,6,5,4,3,2,1,0:T(4,128)(2,1)}, u32[]{:S(2)}) copy-start(bf16[2,1,8,1,4,4,4,1326]{7,6,5,4,3,2,1,0:T(4,128)(2,1)} %param.18) | copy-start | bytes 8146948
  10.8 2.5 copy-start.1
  10.8 2.5 copy-start.2
  10.8 2.5 copy-start.4
  192.2 141.4 %copy-start.3 = (f32[2,1,1326]{2,1,0:T(1,128)}, f32[2,1,1326]{2,1,0:T(1,128)S(1)}, u32[]{:S(2)}) copy-start(f32[2,1,1326]{2,1,0:T(1,128)S(1)} %pmax.7) | copy-start | bytes 31828
where the time goes:
time: 335 us; the launch traced here: 334 us
  blocking collectives  174 us (52%)
  matrix products  76.6 us (23%)
  loops' own time  42.6 us (13%)
  local copies, waits for them, and re-layouts  24.9 us (7%)
  other arithmetic  14.9 us (4%)
    psum x1, blocking collectives, local(): flop_value = lax.psum(jnp.sum(turn_values, axis=1), 'turn') / turn_total  141 us
    dot_general x16, matrix products, showdown(): return jnp.dot(line_reach, payoff, preferred_element_type=jnp.float32)  76.6 us
    another operation x1, loops' own time, board_values(): totals = lax.map(one_board, jnp.arange(flops * boards, dtype=jnp.int32))  42.6 us
    pmax x1, blocking collectives, local(): turn_values = lax.pmax(totals, 'line')  33.1 us
    dynamic_slice x16, local copies, waits for them, and re-layouts, one_board(): strengths[flop_index, board_index]  13.1 us
    dynamic_slice x16, local copies, waits for them, and re-layouts, board_values(): totals = lax.map(one_board, jnp.arange(flops * boards, dtype=jnp.int32))  9.38 us

commit v1 on v0

v1 whole, which is shorter than its diff:
```python
import functools

import jax
import jax.numpy as jnp
import numpy as np
from jax import lax
from jax.experimental import pallas as pl
from jax.experimental.pallas import tpu as pltpu
from jax.sharding import Mesh
from jax.sharding import PartitionSpec as P

CARDS = 52
LANES = 128
F8 = jnp.float8_e4m3fn
F32 = jnp.float32
BF16 = jnp.bfloat16


def hand_cards():
    lower_card, upper_card = np.triu_indices(CARDS, 1)
    return lower_card.astype(np.int32), upper_card.astype(np.int32)


def padded(hands):
    return -(-hands // LANES) * LANES


def holds_rows(hands):
    lower_card, upper_card = hand_cards()
    width = padded(hands)
    holds = np.zeros((64, width), np.float32)
    holds[lower_card, np.arange(hands)] = 1.0
    holds[upper_card, np.arange(hands)] = 1.0
    return holds


def ordered(ranks):
    octave = ranks >> 7
    low = jnp.left_shift(1, jnp.minimum(octave, 29)).astype(F32)
    high = jnp.left_shift(1, jnp.maximum(octave - 29, 0)).astype(F32)
    return ((ranks & 127) + 128).astype(F32) * low * high


def board_kernel(
    flop_cards, turn_cards, river_cards, holds_ref, cards_ref, ranks_ref, flop_reach_ref, turn_ref, stake_ref, river_ref,
    out_ref, mask_ref, strength_ref, column_ref, payoff_ref, *, rivers, hands,
):
    width = padded(hands)
    board = pl.program_id(0)
    flop = board // rivers
    river = lax.rem(board, rivers)
    tiles = [(at, min(256, width - at)) for at in range(0, width, 256)]

    @pl.when(board == 0)
    def _():
        holds = holds_ref[...]
        for at, size in tiles:
            shared = lax.dot_general(holds, holds[:, at:at + size], (((0,), (0,)), ((), ())), preferred_element_type=F32)
            mask_ref[:, at:at + size] = (1.0 - jnp.minimum(shared, 1.0)).astype(BF16)
        strength = ordered(ranks_ref[...])
        pad = jnp.zeros((strength.shape[0], width - hands), F32)
        strength = jnp.concatenate([strength, pad], axis=1)
        for row in range(strength.shape[0]):
            strength_ref[row] = strength[row:row + 1]
        for at in range(0, width, LANES):
            column_ref[at:at + LANES, :] = strength[:, at:at + LANES].T

    lower, upper = cards_ref[0:1, :], cards_ref[1:2, :]

    def clear_of(card):
        return jnp.where((lower == card) | (upper == card), 0.0, 1.0)

    flop_clear = clear_of(flop_cards[flop, 0]) * clear_of(flop_cards[flop, 1]) * clear_of(flop_cards[flop, 2])
    unblocked = flop_clear * clear_of(turn_cards[flop, 0]) * clear_of(river_cards[flop, river])
    opening = flop_reach_ref[flop] * unblocked
    turn = turn_ref[flop].astype(F32)
    turn_prob = turn / jnp.sum(turn, axis=0, keepdims=True)
    weights = river_ref[0].astype(F32)
    total = jnp.sum(weights, axis=1)
    staked = jnp.sum(weights * stake_ref[...], axis=1)
    share = staked / total
    lines = share.reshape(4, 4, hands) * (opening * turn_prob)[:, None, :]
    lines = lines.reshape(16, hands)
    lines = jnp.concatenate([lines, jnp.zeros((16, width - hands), F32)], axis=1)
    parts = lines.astype(BF16)

    columns = column_ref[...]
    lane = lax.broadcasted_iota(jnp.int32, columns.shape, 1)
    column = jnp.sum(jnp.where(lane == board, columns, 0.0), axis=1, keepdims=True)
    column = jnp.broadcast_to(column, (width, LANES)).astype(BF16)
    leaves = []
    for at, size in tiles:
        for part in range(at, at + size, LANES):
            row = strength_ref[board, :, part:part + LANES].astype(BF16)
            mask = mask_ref[:, part:part + LANES]
            sign = jnp.minimum(jnp.maximum(row - column, -mask), mask)
            payoff_ref[:, part:part + LANES] = sign.astype(F8)
        product = jnp.dot(parts, payoff_ref[:, at:at + size], preferred_element_type=F32)
        leaves.append(product)
    leaves = jnp.concatenate(leaves, axis=1)[:, :hands].reshape(4, 4, hands)
    value = jnp.sum(jnp.max(leaves, axis=1), axis=0, keepdims=True) * unblocked

    @pl.when(river == 0)
    def _():
        out_ref[flop] = jnp.zeros((1, hands), F32)

    out_ref[flop] += value


def board_values(flop_cards, turn_cards, river_cards, ranks, flop_reach, turn_policy, river_policy, stake):
    flops, rivers, hands = ranks.shape
    boards = flops * rivers
    width = padded(hands)
    smem = pl.BlockSpec(memory_space=pltpu.SMEM)
    whole = lambda *shape: pl.BlockSpec(shape, lambda b: (0,) * len(shape))
    cards = jnp.asarray(np.stack(hand_cards()))
    return pl.pallas_call(
        functools.partial(board_kernel, rivers=rivers, hands=hands),
        grid=(boards,),
        in_specs=[
            smem, smem, smem,
            whole(64, width), whole(2, hands), whole(boards, hands), whole(flops, 1, hands), whole(flops, 4, hands),
            whole(16, 4, 1),
            pl.BlockSpec((1, 16, 4, hands), lambda b: (b, 0, 0, 0)),
        ],
        out_specs=whole(flops, 1, hands),
        out_shape=jax.ShapeDtypeStruct((flops, 1, hands), F32),
        scratch_shapes=[
            pltpu.VMEM((width, width), BF16),
            pltpu.VMEM((boards, 1, width), F32),
            pltpu.VMEM((width, boards), F32),
            pltpu.VMEM((width, width), F8),
        ],
        compiler_params=pltpu.CompilerParams(vmem_limit_bytes=48 * 2**20),
        name="boards",
    )(
        flop_cards, turn_cards, river_cards, jnp.asarray(holds_rows(hands), BF16), cards, ranks.reshape(boards, hands),
        flop_reach[:, None], turn_policy, stake.reshape(16, 4, 1), river_policy.reshape(boards, 16, 4, hands),
    )


def swap(values, axis, size, flip, combine):
    return combine(values, lax.ppermute(values, axis, [(i, i ^ flip) for i in range(size)]))


def local(flop_cards, turn_cards, river_cards, ranks, flop_reach, turn_policy, river_policy, stake):
    rivers = river_cards.shape[2]
    totals = board_values(
        flop_cards, turn_cards, river_cards[:, 0], ranks[:, 0], flop_reach, turn_policy[:, 0, 0], river_policy[:, 0, :, 0], stake[0]
    )
    values = totals / rivers
    values = swap(values, "z_lo", 2, 1, jnp.maximum)
    values = swap(values, "y", 4, 1, jnp.maximum)
    values = swap(values, "y", 4, 3, jnp.maximum)
    total = swap(values, "core", 2, 1, jnp.add)
    total = swap(total, "x", 4, 1, jnp.add)
    total = swap(total, "x", 4, 3, jnp.add)
    total = swap(total, "z_hi", 4, 1, jnp.add)
    total = swap(total, "z_hi", 4, 3, jnp.add)
    return values, total[:, 0] / 32


def solution(mesh):
    fine = Mesh(mesh.devices.reshape(4, 4, 2, 2, 4), ("z_hi", "x", "core", "z_lo", "y"))
    turn, line = ("z_hi", "x", "core"), ("z_lo", "y")
    in_specs = (
        P(),
        P(None, turn),
        P(None, turn, None),
        P(None, turn, None, None),
        P(),
        P(None, turn, line, None, None),
        P(None, turn, None, line, None, None, None, None),
        P(line, None, None, None),
    )
    out_specs = (P(None, turn, None), P())
    return jax.shard_map(local, mesh=fine, in_specs=in_specs, out_specs=out_specs, check_vma=False)
```

time: 335 us -> 75.4 us (0.23)
  the two profiles are of different devices: /device:TPU:32 before, /device:TPU:6 now
where the time goes in v1:
time: 75.4 us; the launch traced here: 75 us
  Pallas kernels  29.6 us (39%)
  starting transfers between devices  19.5 us (26%)
  waiting for transfers between devices  15.8 us (21%)
  local copies, waits for them, and re-layouts  9.38 us (12%)
    pallas_call x1, Pallas kernels, board_values(): pl.pallas_call(functools.partial(board_kernel, rivers=rivers, hands=hands...  29.6 us
    ppermute x8, starting transfers between devices, swap(): lax.ppermute(values, axis, [(i, i ^ flip) for i in range(size)])  19.5 us
    ppermute x8, waiting for transfers between devices, swap(): lax.ppermute(values, axis, [(i, i ^ flip) for i in range(size)])  15.8 us
    unnamed x18, local copies, waits for them, and re-layouts  7.77 us
  transfers between devices with their start and end apart: 8, of which 8 were waited for; matrix products, arithmetic and copies ran while one was open for 0% of the time, Pallas kernels for 0%

profile of v1, /device:TPU:6, one launch (start us, length us, event | category | flops | bytes accessed | tf_op | source)
XLA Modules:
  0.0 75.0 jit_solution(14849121284404395024)
XLA Ops:
  0.6 0.7 copy.13.turn_cards
  1.4 0.7 broadcast_in_dim.3.flop_reach_ref
  2.1 0.9 %copy.14.stake_ref = f32[16,4,1]{2,1,0:T(4,128)S(1)} copy(f32[16,4,1]{1,0,2:T(8,128)} %bitcast.13) | data formatting | bytes 512 | tf_op jit(solution)/shard_map/reshape;squeeze | solution.py:138
  3.0 0.0 copy-start
  3.0 1.8 %copy-done = bf16[2,1,8,1,4,4,4,1326]{7,6,5,4,3,2,1,0:T(4,128)(2,1)S(1)} copy-done((bf16[2,1,8,1,4,4,4,1326]{7,6,5,4,3,2,1,0:T(4,128)(2,1)S(1)}, bf16[2,1,8,1,4,4,4,1326]{7,6,5,4,3,2,1,0:T(4,128)(2,1)}, u32[]{:S(2)}) %copy-start) | copy-done | bytes 2715672
  4.8 0.0 copy-start.1
  4.8 0.9 %copy-done.1 = bf16[64,1408]{1,0:T(8,128)(2,1)S(1)} copy-done((bf16[64,1408]{1,0:T(8,128)(2,1)S(1)}, bf16[64,1408]{1,0:T(8,128)(2,1)}, u32[]{:S(2)}) %copy-start.1) | copy-done | bytes 180248
  5.7 0.0 copy-start.2
  5.7 0.9 %copy-done.2 = s32[2,1,8,1326]{3,2,1,0:T(8,128)S(1)} copy-done((s32[2,1,8,1326]{3,2,1,0:T(8,128)S(1)}, s32[2,1,8,1326]{3,2,1,0:T(8,128)}, u32[]{:S(2)}) %copy-start.2) | copy-done | bytes 84888
  6.6 0.0 copy-start.3
  6.6 0.7 copy-done.3
  7.3 0.0 copy-start.4
  7.3 0.7 copy-done.4
  8.0 0.0 copy-start.5
  8.0 0.7 copy-done.5
  8.7 0.0 copy-start.6
  8.7 0.7 copy-done.6
  9.4 29.6 %boards.1 = f32[2,1,1326]{2,1,0:T(1,128)S(1)} custom-call(s32[2,3]{1,0:T(2,128)S(1)} %copy-done.5, s32[2,1]{1,0:T(2,128)S(1)} %copy.13.turn_cards, s32[2,8]{1,0:T(2,128)S(1)} %bitcast.11, bf16[64,1408]{1,0:T(8,128)(2,1)S(1)} %copy-done.1, s32[2,1326]{1,0:T(2,128)S(1)} %copy-done.4, s32[16,1326]{1,0:T(8,128)S(1)} %bitcast.9, ...), custom_call_target="tpu_custom_call" | custom-call | tf_op jit(solution)/shard_map/boards/pallas_call | solution.py:117
  39.0 2.0 %collective-permute-start = (f32[2,1,1326]{2,1,0:T(1,128)S(1)}, f32[2,1,1326]{2,1,0:T(1,128)S(1)}, u32[]{:S(2)}, u32[]{:S(2)}) collective-permute-start(f32[2,1,1326]{2,1,0:T(1,128)S(1)} %broadcast_multiply_fusion), channel_id=1, source_target_pairs={{0,4},{4,0},{1,5},{5,1},{2,6},{6,2},{3,7},{7,3},{8,12},{12,8},{9,1... | collective-permute-start | bytes 31832 | tf_op jit(solution)/shard_map/ppermute | solution.py:143
  41.0 1.8 %collective-permute-done = f32[2,1,1326]{2,1,0:T(1,128)S(1)} collective-permute-done((f32[2,1,1326]{2,1,0:T(1,128)S(1)}, f32[2,1,1326]{2,1,0:T(1,128)S(1)}, u32[]{:S(2)}, u32[]{:S(2)}) %collective-permute-start) | collective-permute-done | bytes 10640 | tf_op jit(solution)/shard_map/ppermute | solution.py:143
  42.8 1.7 %collective-permute-start.1 = (f32[2,1,1326]{2,1,0:T(1,128)S(1)}, f32[2,1,1326]{2,1,0:T(1,128)S(1)}, u32[]{:S(2)}, u32[]{:S(2)}) collective-permute-start(f32[2,1,1326]{2,1,0:T(1,128)S(1)} %fusion), channel_id=1, source_target_pairs={{0,1},{1,0},{2,3},{3,2},{4,5},{5,4},{6,7},{7,6},{8,9},{9,8},{10,11... | collective-permute-start | bytes 31832 | tf_op jit(solution)/shard_map/ppermute | solution.py:143
  44.4 2.1 %collective-permute-done.1 = f32[2,1,1326]{2,1,0:T(1,128)S(1)} collective-permute-done((f32[2,1,1326]{2,1,0:T(1,128)S(1)}, f32[2,1,1326]{2,1,0:T(1,128)S(1)}, u32[]{:S(2)}, u32[]{:S(2)}) %collective-permute-start.1) | collective-permute-done | bytes 10640 | tf_op jit(solution)/shard_map/ppermute | solution.py:143
  46.6 3.1 %collective-permute-start.2 = (f32[2,1,1326]{2,1,0:T(1,128)S(1)}, f32[2,1,1326]{2,1,0:T(1,128)S(1)}, u32[]{:S(2)}, u32[]{:S(2)}) collective-permute-start(f32[2,1,1326]{2,1,0:T(1,128)S(1)} %max.10), channel_id=1, source_target_pairs={{0,3},{1,2},{2,1},{3,0},{4,7},{5,6},{6,5},{7,4},{8,11},{9,10},{10,... | collective-permute-start | bytes 31832 | tf_op jit(solution)/shard_map/ppermute | solution.py:143
  49.7 1.9 %collective-permute-done.2 = f32[2,1,1326]{2,1,0:T(1,128)S(1)} collective-permute-done((f32[2,1,1326]{2,1,0:T(1,128)S(1)}, f32[2,1,1326]{2,1,0:T(1,128)S(1)}, u32[]{:S(2)}, u32[]{:S(2)}) %collective-permute-start.2) | collective-permute-done | bytes 10640 | tf_op jit(solution)/shard_map/ppermute | solution.py:143
  51.6 0.0 copy-start.7
  51.6 0.1 collective-permute-start.3
  51.7 1.2 %collective-permute-done.3 = f32[2,1,1326]{2,1,0:T(1,128)S(1)} collective-permute-done((f32[2,1,1326]{2,1,0:T(1,128)S(1)}, f32[2,1,1326]{2,1,0:T(1,128)S(1)}, u32[]{:S(2)}, u32[]{:S(2)}) %collective-permute-start.3) | collective-permute-done | bytes 10640 | tf_op jit(solution)/shard_map/ppermute | solution.py:143
  52.9 0.9 %collective-permute-start.4 = (f32[2,1,1326]{2,1,0:T(1,128)S(1)}, f32[2,1,1326]{2,1,0:T(1,128)S(1)}, u32[]{:S(2)}, u32[]{:S(2)}) collective-permute-start(f32[2,1,1326]{2,1,0:T(1,128)S(1)} %add.15), channel_id=1, source_target_pairs={{0,16},{16,0},{32,48},{48,32},{1,17},{17,1},{33,49},{49,33},{2,18}... | collective-permute-start | bytes 31832 | tf_op jit(solution)/shard_map/ppermute | solution.py:143
  53.8 2.9 %collective-permute-done.4 = f32[2,1,1326]{2,1,0:T(1,128)S(1)} collective-permute-done((f32[2,1,1326]{2,1,0:T(1,128)S(1)}, f32[2,1,1326]{2,1,0:T(1,128)S(1)}, u32[]{:S(2)}, u32[]{:S(2)}) %collective-permute-start.4) | collective-permute-done | bytes 10640 | tf_op jit(solution)/shard_map/ppermute | solution.py:143
  56.7 2.3 %collective-permute-start.5 = (f32[2,1,1326]{2,1,0:T(1,128)S(1)}, f32[2,1,1326]{2,1,0:T(1,128)S(1)}, u32[]{:S(2)}, u32[]{:S(2)}) collective-permute-start(f32[2,1,1326]{2,1,0:T(1,128)S(1)} %add.16), channel_id=1, source_target_pairs={{0,48},{16,32},{32,16},{48,0},{1,49},{17,33},{33,17},{49,1},{2,50}... | collective-permute-start | bytes 31832 | tf_op jit(solution)/shard_map/ppermute | solution.py:143
  59.0 2.7 %collective-permute-done.5 = f32[2,1,1326]{2,1,0:T(1,128)S(1)} collective-permute-done((f32[2,1,1326]{2,1,0:T(1,128)S(1)}, f32[2,1,1326]{2,1,0:T(1,128)S(1)}, u32[]{:S(2)}, u32[]{:S(2)}) %collective-permute-start.5) | collective-permute-done | bytes 10640 | tf_op jit(solution)/shard_map/ppermute | solution.py:143
  61.7 3.4 %collective-permute-start.6 = (f32[2,1,1326]{2,1,0:T(1,128)S(1)}, f32[2,1,1326]{2,1,0:T(1,128)S(1)}, u32[]{:S(2)}, u32[]{:S(2)}) collective-permute-start(f32[2,1,1326]{2,1,0:T(1,128)S(1)} %add.17), channel_id=1, source_target_pairs={{0,64},{64,0},{128,192},{192,128},{1,65},{65,1},{129,193},{193,129... | collective-permute-start | bytes 31832 | tf_op jit(solution)/shard_map/ppermute | solution.py:143
  65.0 1.7 %collective-permute-done.6 = f32[2,1,1326]{2,1,0:T(1,128)S(1)} collective-permute-done((f32[2,1,1326]{2,1,0:T(1,128)S(1)}, f32[2,1,1326]{2,1,0:T(1,128)S(1)}, u32[]{:S(2)}, u32[]{:S(2)}) %collective-permute-start.6) | collective-permute-done | bytes 10640 | tf_op jit(solution)/shard_map/ppermute | solution.py:143
  66.7 6.0 %collective-permute-start.7 = (f32[2,1,1326]{2,1,0:T(1,128)S(1)}, f32[2,1,1326]{2,1,0:T(1,128)S(1)}, u32[]{:S(2)}, u32[]{:S(2)}) collective-permute-start(f32[2,1,1326]{2,1,0:T(1,128)S(1)} %add.18), channel_id=1, source_target_pairs={{0,192},{64,128},{128,64},{192,0},{1,193},{65,129},{129,65},{193,1... | collective-permute-start | bytes 31832 | tf_op jit(solution)/shard_map/ppermute | solution.py:143
  72.7 1.7 %collective-permute-done.7 = f32[2,1,1326]{2,1,0:T(1,128)S(1)} collective-permute-done((f32[2,1,1326]{2,1,0:T(1,128)S(1)}, f32[2,1,1326]{2,1,0:T(1,128)S(1)}, u32[]{:S(2)}, u32[]{:S(2)}) %collective-permute-start.7) | collective-permute-done | bytes 10640 | tf_op jit(solution)/shard_map/ppermute | solution.py:143
  74.4 0.6 copy.19
  75.0 0.0 copy-done.7
  (9 shorter events, 0.1 us)
Async XLA Ops:
  3.0 1.8 %copy-start = (bf16[2,1,8,1,4,4,4,1326]{7,6,5,4,3,2,1,0:T(4,128)(2,1)S(1)}, bf16[2,1,8,1,4,4,4,1326]{7,6,5,4,3,2,1,0:T(4,128)(2,1)}, u32[]{:S(2)}) copy-start(bf16[2,1,8,1,4,4,4,1326]{7,6,5,4,3,2,1,0:T(4,128)(2,1)} %param.16) | copy-start | bytes 8146948
  4.8 0.9 %copy-start.1 = (bf16[64,1408]{1,0:T(8,128)(2,1)S(1)}, bf16[64,1408]{1,0:T(8,128)(2,1)}, u32[]{:S(2)}) copy-start(bf16[64,1408]{1,0:T(8,128)(2,1)} %constant.11.clone.holds_ref) | copy-start | bytes 540676
  5.7 0.9 %copy-start.2 = (s32[2,1,8,1326]{3,2,1,0:T(8,128)S(1)}, s32[2,1,8,1326]{3,2,1,0:T(8,128)}, u32[]{:S(2)}) copy-start(s32[2,1,8,1326]{3,2,1,0:T(8,128)} %param.13) | copy-start | bytes 254596
  6.6 0.7 copy-start.3
  7.3 0.7 copy-start.4
  8.0 0.7 copy-start.5
  8.7 0.7 copy-start.6
  39.0 3.8 %collective-permute-start = (f32[2,1,1326]{2,1,0:T(1,128)S(1)}, f32[2,1,1326]{2,1,0:T(1,128)S(1)}, u32[]{:S(2)}, u32[]{:S(2)}) collective-permute-start(f32[2,1,1326]{2,1,0:T(1,128)S(1)} %broadcast_multiply_fusion), channel_id=1, source_target_pairs={{0,4},{4,0},{1,5},{5,1},{2,6},{6,2},{3,7},{7,3},{8,12},{12,8},{9,1... | collective-permute-start | bytes 31832 | tf_op jit(solution)/shard_map/ppermute | solution.py:143
  42.8 3.8 %collective-permute-start.1 = (f32[2,1,1326]{2,1,0:T(1,128)S(1)}, f32[2,1,1326]{2,1,0:T(1,128)S(1)}, u32[]{:S(2)}, u32[]{:S(2)}) collective-permute-start(f32[2,1,1326]{2,1,0:T(1,128)S(1)} %fusion), channel_id=1, source_target_pairs={{0,1},{1,0},{2,3},{3,2},{4,5},{5,4},{6,7},{7,6},{8,9},{9,8},{10,11... | collective-permute-start | bytes 31832 | tf_op jit(solution)/shard_map/ppermute | solution.py:143
  46.6 5.0 %collective-permute-start.2 = (f32[2,1,1326]{2,1,0:T(1,128)S(1)}, f32[2,1,1326]{2,1,0:T(1,128)S(1)}, u32[]{:S(2)}, u32[]{:S(2)}) collective-permute-start(f32[2,1,1326]{2,1,0:T(1,128)S(1)} %max.10), channel_id=1, source_target_pairs={{0,3},{1,2},{2,1},{3,0},{4,7},{5,6},{6,5},{7,4},{8,11},{9,10},{10,... | collective-permute-start | bytes 31832 | tf_op jit(solution)/shard_map/ppermute | solution.py:143
  51.6 23.4 %copy-start.7 = (f32[2,1,1326]{2,1,0:T(1,128)}, f32[2,1,1326]{2,1,0:T(1,128)S(1)}, u32[]{:S(2)}) copy-start(f32[2,1,1326]{2,1,0:T(1,128)S(1)} %max.11) | copy-start | bytes 31828
  51.6 1.3 %collective-permute-start.3 = (f32[2,1,1326]{2,1,0:T(1,128)S(1)}, f32[2,1,1326]{2,1,0:T(1,128)S(1)}, u32[]{:S(2)}, u32[]{:S(2)}) collective-permute-start(f32[2,1,1326]{2,1,0:T(1,128)S(1)} %max.11), channel_id=1, source_target_pairs={{0,8},{8,0},{1,9},{9,1},{2,10},{10,2},{3,11},{11,3},{4,12},{12,4},... | collective-permute-start | bytes 31832 | tf_op jit(solution)/shard_map/ppermute | solution.py:143
  52.9 3.8 %collective-permute-start.4 = (f32[2,1,1326]{2,1,0:T(1,128)S(1)}, f32[2,1,1326]{2,1,0:T(1,128)S(1)}, u32[]{:S(2)}, u32[]{:S(2)}) collective-permute-start(f32[2,1,1326]{2,1,0:T(1,128)S(1)} %add.15), channel_id=1, source_target_pairs={{0,16},{16,0},{32,48},{48,32},{1,17},{17,1},{33,49},{49,33},{2,18}... | collective-permute-start | bytes 31832 | tf_op jit(solution)/shard_map/ppermute | solution.py:143
  56.7 5.0 %collective-permute-start.5 = (f32[2,1,1326]{2,1,0:T(1,128)S(1)}, f32[2,1,1326]{2,1,0:T(1,128)S(1)}, u32[]{:S(2)}, u32[]{:S(2)}) collective-permute-start(f32[2,1,1326]{2,1,0:T(1,128)S(1)} %add.16), channel_id=1, source_target_pairs={{0,48},{16,32},{32,16},{48,0},{1,49},{17,33},{33,17},{49,1},{2,50}... | collective-permute-start | bytes 31832 | tf_op jit(solution)/shard_map/ppermute | solution.py:143
  61.7 5.0 %collective-permute-start.6 = (f32[2,1,1326]{2,1,0:T(1,128)S(1)}, f32[2,1,1326]{2,1,0:T(1,128)S(1)}, u32[]{:S(2)}, u32[]{:S(2)}) collective-permute-start(f32[2,1,1326]{2,1,0:T(1,128)S(1)} %add.17), channel_id=1, source_target_pairs={{0,64},{64,0},{128,192},{192,128},{1,65},{65,1},{129,193},{193,129... | collective-permute-start | bytes 31832 | tf_op jit(solution)/shard_map/ppermute | solution.py:143
  66.7 7.7 %collective-permute-start.7 = (f32[2,1,1326]{2,1,0:T(1,128)S(1)}, f32[2,1,1326]{2,1,0:T(1,128)S(1)}, u32[]{:S(2)}, u32[]{:S(2)}) collective-permute-start(f32[2,1,1326]{2,1,0:T(1,128)S(1)} %add.18), channel_id=1, source_target_pairs={{0,192},{64,128},{128,64},{192,0},{1,193},{65,129},{129,65},{193,1... | collective-permute-start | bytes 31832 | tf_op jit(solution)/shard_map/ppermute | solution.py:143

commit v2 on v1

v2 whole, which is shorter than its diff:
```python
import functools

import jax
import jax.numpy as jnp
from jax import lax
from jax.experimental import pallas as pl
from jax.experimental.pallas import tpu as pltpu
from jax.sharding import Mesh
from jax.sharding import PartitionSpec as P

CARDS = 52
LANES = 128
F8 = jnp.float8_e4m3fn
F32 = jnp.float32
BF16 = jnp.bfloat16
GROUP = 4
DEPTH = 256


def padded(hands):
    return -(-hands // LANES) * LANES


def hand_cards(width):
    hand = lax.broadcasted_iota(jnp.int32, (1, width), 1)

    def first_of(lower):
        return (lower * (2 * CARDS - 1 - lower)) >> 1

    root = jnp.sqrt(jnp.maximum(((2 * CARDS - 1) ** 2 - 8 * hand).astype(F32), 0.0))
    lower = ((2 * CARDS - 1 - root) * 0.5).astype(jnp.int32)
    lower = lower + (first_of(lower + 1) <= hand).astype(jnp.int32)
    lower = lower - (first_of(lower) > hand).astype(jnp.int32)
    return lower, hand - first_of(lower) + lower + 1


def ordered(ranks):
    octave = ranks >> 7
    low = jnp.left_shift(1, jnp.minimum(octave, 29)).astype(F32)
    high = jnp.left_shift(1, jnp.maximum(octave - 29, 0)).astype(F32)
    return ((ranks & 127) + 128).astype(F32) * low * high


def board_kernel(
    flop_cards_in, turn_cards_in, river_cards_in, ranks_in, flop_reach_in, turn_in, stake_in, river_in, out_ref,
    flop_cards, turn_cards, river_cards, ranks_ref, flop_reach_ref, turn_ref, stake_ref, river_ref,
    free_ref, minus_ref, rows_ref, columns_ref, clear_ref, entry_ref, payoff_ref, leaves_ref, sems, river_sems, *, hands,
):
    flops, rivers = river_cards.shape
    boards = flops * rivers
    width = padded(hands)
    group = GROUP
    tiles = [(at, min(256, width - at)) for at in range(0, width, 256)]
    pairs = [
        (flop_cards_in, flop_cards), (turn_cards_in, turn_cards), (river_cards_in, river_cards), (ranks_in, ranks_ref),
        (flop_reach_in, flop_reach_ref), (turn_in, turn_ref), (stake_in, stake_ref),
    ]
    copies = [pltpu.make_async_copy(source, target, sems.at[i]) for i, (source, target) in enumerate(pairs)]
    for copy in copies:
        copy.start()

    def river_copy(board):
        return pltpu.make_async_copy(river_in.at[board], river_ref.at[board], river_sems.at[board])

    for board in range(boards):
        river_copy(board).start()

    lower, upper = hand_cards(width)
    card = lax.broadcasted_iota(jnp.int32, (64, width), 0)
    holds = jnp.where((card == lower) | (card == upper), 1.0, 0.0).astype(BF16)
    for at, size in tiles:
        shared = lax.dot_general(holds, holds[:, at:at + size], (((0,), (0,)), ((), ())), preferred_element_type=F32)
        free = jnp.maximum(1.0 - shared, 0.0).astype(BF16)
        free_ref[:, at:at + size] = free
        minus_ref[:, at:at + size] = -free
    for copy in copies:
        copy.wait()
    strength = ordered(ranks_ref[...])
    strength = jnp.concatenate([strength, jnp.zeros((boards, width - hands), F32)], axis=1)
    for row in range(boards):
        rows_ref[row] = jnp.broadcast_to(strength[row:row + 1], (16, width)).astype(BF16)
    for at in range(0, width, LANES):
        for first in range(0, boards, group):
            columns_ref[first // group, at:at + LANES, :] = strength[first:first + group, at:at + LANES].T

    def clear_of(card):
        return jnp.where((lower == card) | (upper == card), 0.0, 1.0)

    def widen(values):
        return jnp.concatenate([values, jnp.zeros((values.shape[0], width - hands), F32)], axis=1)

    for flop in range(flops):
        clear = clear_of(turn_cards[flop])
        for i in range(3):
            clear = clear * clear_of(flop_cards[flop, i])
        clear_ref[flop] = clear
        turn = turn_ref[flop].astype(F32)
        turn_prob = turn / jnp.sum(turn, axis=0, keepdims=True)
        entry_ref[flop] = widen(flop_reach_ref[flop:flop + 1, :] * turn_prob) * clear

    stake16 = stake_ref[...].reshape(16, 4)
    lane = lax.broadcasted_iota(jnp.int32, (16, 64), 1)
    own = (lane >> 2) == lax.broadcasted_iota(jnp.int32, (16, 64), 0)
    pots = jnp.zeros((16, 64), F32)
    for reply in range(4):
        pots = jnp.where((lane & 3) == reply, stake16[:, reply:reply + 1], pots)
    pots = jnp.where(own, pots, 0.0)
    coarse = pots.astype(BF16)
    spread = jnp.concatenate([own.astype(BF16), coarse, (pots - coarse.astype(F32)).astype(BF16)], axis=0)

    def one_group(at_group, acc):
        first = at_group * group
        flop = first // rivers
        lines, clears = [], []
        for i in range(group):
            river_copy(first + i).wait()
        for i in range(group):
            sums = jnp.dot(spread, river_ref[first + i].reshape(64, hands), preferred_element_type=F32)
            share = (sums[16:32] + sums[32:48]) / sums[:16]
            clear = clear_of(river_cards[flop, lax.rem(first + i, rivers)])
            reach = share.reshape(4, 4, hands) * (entry_ref[flop] * clear)[:, None, :hands]
            lines.append(widen(reach.reshape(16, hands)).astype(BF16))
            clears.append(clear)
        for chunk in range(0, width, DEPTH):
            stop = min(chunk + DEPTH, width)
            for down in range(chunk, stop, 32):
                column = [
                    jnp.broadcast_to(columns_ref[at_group, down:down + 32, i:i + 1], (32, LANES)).astype(BF16)
                    for i in range(group)
                ]
                for at in range(0, width, LANES):
                    free = free_ref[down:down + 32, at:at + LANES]
                    minus = minus_ref[down:down + 32, at:at + LANES]
                    for i in range(group):
                        row = rows_ref[first + i, :, at:at + LANES]
                        gap = jnp.concatenate([row, row], axis=0) - column[i]
                        payoff_ref[i, down:down + 32, at:at + LANES] = jnp.minimum(jnp.maximum(gap, minus), free).astype(F8)
            for i in range(group):
                product = jnp.dot(lines[i][:, chunk:stop], payoff_ref[i, chunk:stop, :], preferred_element_type=F32)
                if chunk == 0:
                    leaves_ref[i] = product
                else:
                    leaves_ref[i] += product
        value = jnp.zeros((1, width), F32)
        for i in range(group):
            best = jnp.max(leaves_ref[i].reshape(4, 4, width), axis=1)
            value = value + jnp.sum(best, axis=0, keepdims=True) * clears[i]
        return acc + value

    groups = rivers // group
    for flop in range(flops):
        value = lax.fori_loop(flop * groups, (flop + 1) * groups, one_group, jnp.zeros((1, width), F32))
        out_ref[flop:flop + 1, :] = (value * clear_ref[flop] * (1 / rivers))[:, :hands]


def board_values(flop_cards, turn_cards, river_cards, ranks, flop_reach, turn_policy, river_policy, stake):
    flops, rivers, hands = ranks.shape
    boards = flops * rivers
    width = padded(hands)
    args = (
        flop_cards, turn_cards, river_cards, ranks.reshape(boards, hands), flop_reach, turn_policy, stake,
        river_policy.reshape(boards, 16, 4, hands),
    )
    held = [(pltpu.SMEM if i < 3 else pltpu.VMEM)(a.shape, a.dtype) for i, a in enumerate(args)]
    return pl.pallas_call(
        functools.partial(board_kernel, hands=hands),
        in_specs=[pl.BlockSpec(memory_space=pl.ANY)] * len(args),
        out_specs=pl.BlockSpec(memory_space=pltpu.VMEM),
        out_shape=jax.ShapeDtypeStruct((flops, hands), F32),
        scratch_shapes=held + [
            pltpu.VMEM((width, width), BF16),
            pltpu.VMEM((width, width), BF16),
            pltpu.VMEM((boards, 16, width), BF16),
            pltpu.VMEM((boards // GROUP, width, GROUP), F32),
            pltpu.VMEM((flops, 1, width), F32),
            pltpu.VMEM((flops, 4, width), F32),
            pltpu.VMEM((GROUP, width, width), F8),
            pltpu.VMEM((GROUP, 16, width), F32),
            pltpu.SemaphoreType.DMA((len(args) - 1,)),
            pltpu.SemaphoreType.DMA((boards,)),
        ],
        compiler_params=pltpu.CompilerParams(vmem_limit_bytes=56 * 2**20),
        name="boards",
    )(*args)


def swap(values, axis, size, flip, combine):
    return combine(values, lax.ppermute(values, axis, [(i, i ^ flip) for i in range(size)]))


def local(flop_cards, turn_cards, river_cards, ranks, flop_reach, turn_policy, river_policy, stake):
    values = board_values(
        flop_cards, turn_cards[:, 0], river_cards[:, 0], ranks[:, 0], flop_reach, turn_policy[:, 0, 0],
        river_policy[:, 0, :, 0], stake[0]
    )
    values = swap(values, "z_lo", 2, 1, jnp.maximum)
    values = swap(values, "y", 4, 1, jnp.maximum)
    values = swap(values, "y", 4, 3, jnp.maximum)
    total = swap(values, "core", 2, 1, jnp.add)
    total = swap(total, "x", 4, 1, jnp.add)
    total = swap(total, "x", 4, 3, jnp.add)
    total = swap(total, "z_hi", 4, 1, jnp.add)
    total = swap(total, "z_hi", 4, 3, jnp.add)
    return values[:, None, :], total / 32


def solution(mesh):
    fine = Mesh(mesh.devices.reshape(4, 4, 2, 2, 4), ("z_hi", "x", "core", "z_lo", "y"))
    turn, line = ("z_hi", "x", "core"), ("z_lo", "y")
    in_specs = (
        P(),
        P(None, turn),
        P(None, turn, None),
        P(None, turn, None, None),
        P(),
        P(None, turn, line, None, None),
        P(None, turn, None, line, None, None, None, None),
        P(line, None, None, None),
    )
    out_specs = (P(None, turn, None), P())
    return jax.shard_map(local, mesh=fine, in_specs=in_specs, out_specs=out_specs, check_vma=False)
```

time: 75.4 us -> 51.3 us (0.68)
  Pallas kernels: 29.6 us -> 13.7 us
  local copies, waits for them, and re-layouts: 9.38 us -> 0.61 us
  other arithmetic: 0.13 us -> 1.36 us
    pallas_call x1, Pallas kernels: 29.6 us -> 13.7 us  [board_values(): pl.pallas_call(functools.partial(board_kernel, hands=hands), in_specs=[pl...]
    unnamed x18 -> x1, local copies, waits for them, and re-layouts: 7.77 us -> 0.61 us
    another operation x1 -> x0, local copies, waits for them, and re-layouts: 0.89 us -> none  [board_values(): stake.reshape(16, 4, 1)]
  transfers between devices with their start and end apart: 8 -> 8, of which waited for: 8 -> 8; matrix products, arithmetic and copies ran while one was open for 0% -> 1% of each run, Pallas kernels for 0% -> 0%
where the time goes in v2:
time: 51.3 us; the launch traced here: 51.1 us
  starting transfers between devices  19.3 us (38%)
  waiting for transfers between devices  15.4 us (30%)
  Pallas kernels  13.7 us (27%)
  other arithmetic  1.36 us (3%)
  between operations  0.66 us (1%)
  local copies, waits for them, and re-layouts  0.61 us (1%)
    ppermute x8, starting transfers between devices, swap(): lax.ppermute(values, axis, [(i, i ^ flip) for i in range(size)])  19.3 us
    ppermute x8, waiting for transfers between devices, swap(): lax.ppermute(values, axis, [(i, i ^ flip) for i in range(size)])  15.4 us
    pallas_call x1, Pallas kernels, board_values(): pl.pallas_call(functools.partial(board_kernel, hands=hands), in_specs=[pl...  13.7 us
  transfers between devices with their start and end apart: 8, of which 8 were waited for; matrix products, arithmetic and copies ran while one was open for 1% of the time, Pallas kernels for 0%

profile of v2, /device:TPU:6, one launch (start us, length us, event | category | flops | bytes accessed | tf_op | source)
XLA Modules:
  0.0 51.1 jit_solution(12702701492312128459)
XLA Ops:
  0.6 13.7 %boards.1 = f32[2,1326]{1,0:T(2,128)} custom-call(s32[2,3]{1,0:T(2,128)} %flop_cards_in.1, s32[2]{0:T(128)} %bitcast.13, s32[2,8]{1,0:T(2,128)} %bitcast.12, s32[16,1326]{1,0:T(8,128)} %bitcast.9, f32[2,1326]{1,0:T(2,128)} %flop_reach_in.1, bf16[2,4,1326]{2,1,0:T(4,128)(2,1)} %bitcast.10, f32[4,4,4]{2,1,0:T(4,128)} %bitcast.11, bf16[16,16,4,1326]{3,2,1,0:T(4,128)(2,1)} %bitcast.7), custom_call_target="tpu_custom_call" | custom-call | tf_op jit(solution)/shard_map/boards/pallas_call | solution.py:165
  14.4 2.0 %collective-permute-start = (f32[2,1326]{1,0:T(2,128)}, f32[2,1326]{1,0:T(2,128)S(1)}, u32[]{:S(2)}, u32[]{:S(2)}) collective-permute-start(f32[2,1326]{1,0:T(2,128)} %boards.1), channel_id=1, source_target_pairs={{0,4},{4,0},{1,5},{5,1},{2,6},{6,2},{3,7},{7,3},{8,12},{12,8},{9,1... | collective-permute-start | bytes 31832 | tf_op jit(solution)/shard_map/ppermute | solution.py:188
  16.4 2.0 %collective-permute-done = f32[2,1326]{1,0:T(2,128)S(1)} collective-permute-done((f32[2,1326]{1,0:T(2,128)}, f32[2,1326]{1,0:T(2,128)S(1)}, u32[]{:S(2)}, u32[]{:S(2)}) %collective-permute-start) | collective-permute-done | bytes 10640 | tf_op jit(solution)/shard_map/ppermute | solution.py:188
  18.4 0.7 %max.9 = f32[2,1326]{1,0:T(2,128)S(1)} maximum(f32[2,1326]{1,0:T(2,128)} %boards.1, f32[2,1326]{1,0:T(2,128)S(1)} %collective-permute-done) | non-fusion elementwise | flops 2652 | bytes 31824 | tf_op jit(solution)/shard_map/max | solution.py:188
  19.1 1.6 %collective-permute-start.1 = (f32[2,1326]{1,0:T(2,128)S(1)}, f32[2,1326]{1,0:T(2,128)S(1)}, u32[]{:S(2)}, u32[]{:S(2)}) collective-permute-start(f32[2,1326]{1,0:T(2,128)S(1)} %max.9), channel_id=1, source_target_pairs={{0,1},{1,0},{2,3},{3,2},{4,5},{5,4},{6,7},{7,6},{8,9},{9,8},{10,11... | collective-permute-start | bytes 31832 | tf_op jit(solution)/shard_map/ppermute | solution.py:188
  20.7 2.1 %collective-permute-done.1 = f32[2,1326]{1,0:T(2,128)S(1)} collective-permute-done((f32[2,1326]{1,0:T(2,128)S(1)}, f32[2,1326]{1,0:T(2,128)S(1)}, u32[]{:S(2)}, u32[]{:S(2)}) %collective-permute-start.1) | collective-permute-done | bytes 10640 | tf_op jit(solution)/shard_map/ppermute | solution.py:188
  22.8 3.1 %collective-permute-start.2 = (f32[2,1326]{1,0:T(2,128)S(1)}, f32[2,1326]{1,0:T(2,128)S(1)}, u32[]{:S(2)}, u32[]{:S(2)}) collective-permute-start(f32[2,1326]{1,0:T(2,128)S(1)} %max.10), channel_id=1, source_target_pairs={{0,3},{1,2},{2,1},{3,0},{4,7},{5,6},{6,5},{7,4},{8,11},{9,10},{10,... | collective-permute-start | bytes 31832 | tf_op jit(solution)/shard_map/ppermute | solution.py:188
  25.9 1.9 %collective-permute-done.2 = f32[2,1326]{1,0:T(2,128)S(1)} collective-permute-done((f32[2,1326]{1,0:T(2,128)S(1)}, f32[2,1326]{1,0:T(2,128)S(1)}, u32[]{:S(2)}, u32[]{:S(2)}) %collective-permute-start.2) | collective-permute-done | bytes 10640 | tf_op jit(solution)/shard_map/ppermute | solution.py:188
  27.8 0.1 collective-permute-start.3
  27.9 1.2 %collective-permute-done.3 = f32[2,1326]{1,0:T(2,128)S(1)} collective-permute-done((f32[2,1326]{1,0:T(2,128)S(1)}, f32[2,1326]{1,0:T(2,128)S(1)}, u32[]{:S(2)}, u32[]{:S(2)}) %collective-permute-start.3) | collective-permute-done | bytes 10640 | tf_op jit(solution)/shard_map/ppermute | solution.py:188
  29.0 0.9 %collective-permute-start.4 = (f32[2,1326]{1,0:T(2,128)S(1)}, f32[2,1326]{1,0:T(2,128)S(1)}, u32[]{:S(2)}, u32[]{:S(2)}) collective-permute-start(f32[2,1326]{1,0:T(2,128)S(1)} %add.15), channel_id=1, source_target_pairs={{0,16},{16,0},{32,48},{48,32},{1,17},{17,1},{33,49},{49,33},{2,18}... | collective-permute-start | bytes 31832 | tf_op jit(solution)/shard_map/ppermute | solution.py:188
  29.9 2.9 %collective-permute-done.4 = f32[2,1326]{1,0:T(2,128)S(1)} collective-permute-done((f32[2,1326]{1,0:T(2,128)S(1)}, f32[2,1326]{1,0:T(2,128)S(1)}, u32[]{:S(2)}, u32[]{:S(2)}) %collective-permute-start.4) | collective-permute-done | bytes 10640 | tf_op jit(solution)/shard_map/ppermute | solution.py:188
  32.8 2.3 %collective-permute-start.5 = (f32[2,1326]{1,0:T(2,128)S(1)}, f32[2,1326]{1,0:T(2,128)S(1)}, u32[]{:S(2)}, u32[]{:S(2)}) collective-permute-start(f32[2,1326]{1,0:T(2,128)S(1)} %add.16), channel_id=1, source_target_pairs={{0,48},{16,32},{32,16},{48,0},{1,49},{17,33},{33,17},{49,1},{2,50}... | collective-permute-start | bytes 31832 | tf_op jit(solution)/shard_map/ppermute | solution.py:188
  35.1 2.7 %collective-permute-done.5 = f32[2,1326]{1,0:T(2,128)S(1)} collective-permute-done((f32[2,1326]{1,0:T(2,128)S(1)}, f32[2,1326]{1,0:T(2,128)S(1)}, u32[]{:S(2)}, u32[]{:S(2)}) %collective-permute-start.5) | collective-permute-done | bytes 10640 | tf_op jit(solution)/shard_map/ppermute | solution.py:188
  37.8 3.4 %collective-permute-start.6 = (f32[2,1326]{1,0:T(2,128)S(1)}, f32[2,1326]{1,0:T(2,128)S(1)}, u32[]{:S(2)}, u32[]{:S(2)}) collective-permute-start(f32[2,1326]{1,0:T(2,128)S(1)} %add.17), channel_id=1, source_target_pairs={{0,64},{64,0},{128,192},{192,128},{1,65},{65,1},{129,193},{193,129... | collective-permute-start | bytes 31832 | tf_op jit(solution)/shard_map/ppermute | solution.py:188
  41.1 1.7 %collective-permute-done.6 = f32[2,1326]{1,0:T(2,128)S(1)} collective-permute-done((f32[2,1326]{1,0:T(2,128)S(1)}, f32[2,1326]{1,0:T(2,128)S(1)}, u32[]{:S(2)}, u32[]{:S(2)}) %collective-permute-start.6) | collective-permute-done | bytes 10640 | tf_op jit(solution)/shard_map/ppermute | solution.py:188
  42.8 6.0 %collective-permute-start.7 = (f32[2,1326]{1,0:T(2,128)S(1)}, f32[2,1326]{1,0:T(2,128)S(1)}, u32[]{:S(2)}, u32[]{:S(2)}) collective-permute-start(f32[2,1326]{1,0:T(2,128)S(1)} %add.18), channel_id=1, source_target_pairs={{0,192},{64,128},{128,64},{192,0},{1,193},{65,129},{129,65},{193,1... | collective-permute-start | bytes 31832 | tf_op jit(solution)/shard_map/ppermute | solution.py:188
  48.8 0.6 %copy.10 = f32[2,1,1326]{2,1,0:T(1,128)} copy(f32[2,1,1326]{2,0,1:T(2,128)S(1)} %bitcast.8) | data formatting | bytes 21216
  49.5 1.1 %collective-permute-done.7 = f32[2,1326]{1,0:T(2,128)S(1)} collective-permute-done((f32[2,1326]{1,0:T(2,128)S(1)}, f32[2,1326]{1,0:T(2,128)S(1)}, u32[]{:S(2)}, u32[]{:S(2)}) %collective-permute-start.7) | collective-permute-done | bytes 10640 | tf_op jit(solution)/shard_map/ppermute | solution.py:188
  50.5 0.6 %add_multiply_fusion = f32[2,1326]{1,0:T(2,128)} fusion(f32[2,1326]{1,0:T(2,128)S(1)} %add.18, f32[2,1326]{1,0:T(2,128)S(1)} %collective-permute-done.7), kind=kLoop, calls=%fused_computation | loop fusion | flops 5304 | bytes 31824 | tf_op jit(solution)/shard_map/div | solution.py:204
  (6 shorter events, 0.0 us)
Async XLA Ops:
  14.4 4.0 %collective-permute-start = (f32[2,1326]{1,0:T(2,128)}, f32[2,1326]{1,0:T(2,128)S(1)}, u32[]{:S(2)}, u32[]{:S(2)}) collective-permute-start(f32[2,1326]{1,0:T(2,128)} %boards.1), channel_id=1, source_target_pairs={{0,4},{4,0},{1,5},{5,1},{2,6},{6,2},{3,7},{7,3},{8,12},{12,8},{9,1... | collective-permute-start | bytes 31832 | tf_op jit(solution)/shard_map/ppermute | solution.py:188
  19.1 3.7 %collective-permute-start.1 = (f32[2,1326]{1,0:T(2,128)S(1)}, f32[2,1326]{1,0:T(2,128)S(1)}, u32[]{:S(2)}, u32[]{:S(2)}) collective-permute-start(f32[2,1326]{1,0:T(2,128)S(1)} %max.9), channel_id=1, source_target_pairs={{0,1},{1,0},{2,3},{3,2},{4,5},{5,4},{6,7},{7,6},{8,9},{9,8},{10,11... | collective-permute-start | bytes 31832 | tf_op jit(solution)/shard_map/ppermute | solution.py:188
  22.8 5.0 %collective-permute-start.2 = (f32[2,1326]{1,0:T(2,128)S(1)}, f32[2,1326]{1,0:T(2,128)S(1)}, u32[]{:S(2)}, u32[]{:S(2)}) collective-permute-start(f32[2,1326]{1,0:T(2,128)S(1)} %max.10), channel_id=1, source_target_pairs={{0,3},{1,2},{2,1},{3,0},{4,7},{5,6},{6,5},{7,4},{8,11},{9,10},{10,... | collective-permute-start | bytes 31832 | tf_op jit(solution)/shard_map/ppermute | solution.py:188
  27.8 1.3 %collective-permute-start.3 = (f32[2,1326]{1,0:T(2,128)S(1)}, f32[2,1326]{1,0:T(2,128)S(1)}, u32[]{:S(2)}, u32[]{:S(2)}) collective-permute-start(f32[2,1326]{1,0:T(2,128)S(1)} %max.11), channel_id=1, source_target_pairs={{0,8},{8,0},{1,9},{9,1},{2,10},{10,2},{3,11},{11,3},{4,12},{12,4},... | collective-permute-start | bytes 31832 | tf_op jit(solution)/shard_map/ppermute | solution.py:188
  29.0 3.8 %collective-permute-start.4 = (f32[2,1326]{1,0:T(2,128)S(1)}, f32[2,1326]{1,0:T(2,128)S(1)}, u32[]{:S(2)}, u32[]{:S(2)}) collective-permute-start(f32[2,1326]{1,0:T(2,128)S(1)} %add.15), channel_id=1, source_target_pairs={{0,16},{16,0},{32,48},{48,32},{1,17},{17,1},{33,49},{49,33},{2,18}... | collective-permute-start | bytes 31832 | tf_op jit(solution)/shard_map/ppermute | solution.py:188
  32.8 5.0 %collective-permute-start.5 = (f32[2,1326]{1,0:T(2,128)S(1)}, f32[2,1326]{1,0:T(2,128)S(1)}, u32[]{:S(2)}, u32[]{:S(2)}) collective-permute-start(f32[2,1326]{1,0:T(2,128)S(1)} %add.16), channel_id=1, source_target_pairs={{0,48},{16,32},{32,16},{48,0},{1,49},{17,33},{33,17},{49,1},{2,50}... | collective-permute-start | bytes 31832 | tf_op jit(solution)/shard_map/ppermute | solution.py:188
  37.8 5.0 %collective-permute-start.6 = (f32[2,1326]{1,0:T(2,128)S(1)}, f32[2,1326]{1,0:T(2,128)S(1)}, u32[]{:S(2)}, u32[]{:S(2)}) collective-permute-start(f32[2,1326]{1,0:T(2,128)S(1)} %add.17), channel_id=1, source_target_pairs={{0,64},{64,0},{128,192},{192,128},{1,65},{65,1},{129,193},{193,129... | collective-permute-start | bytes 31832 | tf_op jit(solution)/shard_map/ppermute | solution.py:188
  42.8 7.7 %collective-permute-start.7 = (f32[2,1326]{1,0:T(2,128)S(1)}, f32[2,1326]{1,0:T(2,128)S(1)}, u32[]{:S(2)}, u32[]{:S(2)}) collective-permute-start(f32[2,1326]{1,0:T(2,128)S(1)} %add.18), channel_id=1, source_target_pairs={{0,192},{64,128},{128,64},{192,0},{1,193},{65,129},{129,65},{193,1... | collective-permute-start | bytes 31832 | tf_op jit(solution)/shard_map/ppermute | solution.py:188

commit v3 on v2

--- a/solution.py
+++ b/solution.py
@@ -44,7 +44,7 @@
 def board_kernel(
     flop_cards_in, turn_cards_in, river_cards_in, ranks_in, flop_reach_in, turn_in, stake_in, river_in, out_ref,
     flop_cards, turn_cards, river_cards, ranks_ref, flop_reach_ref, turn_ref, stake_ref, river_ref,
-    free_ref, minus_ref, rows_ref, columns_ref, clear_ref, entry_ref, payoff_ref, leaves_ref, sems, river_sems, *, hands,
+    free_ref, rows_ref, columns_ref, wide_ref, clear_ref, entry_ref, payoff_ref, leaves_ref, sems, river_sems, *, hands,
 ):
     flops, rivers = river_cards.shape
     boards = flops * rivers
@@ -72,7 +72,6 @@
         shared = lax.dot_general(holds, holds[:, at:at + size], (((0,), (0,)), ((), ())), preferred_element_type=F32)
         free = jnp.maximum(1.0 - shared, 0.0).astype(BF16)
         free_ref[:, at:at + size] = free
-        minus_ref[:, at:at + size] = -free
     for copy in copies:
         copy.wait()
     strength = ordered(ranks_ref[...])
@@ -80,8 +79,13 @@
     for row in range(boards):
         rows_ref[row] = jnp.broadcast_to(strength[row:row + 1], (16, width)).astype(BF16)
     for at in range(0, width, LANES):
-        for first in range(0, boards, group):
-            columns_ref[first // group, at:at + LANES, :] = strength[first:first + group, at:at + LANES].T
+        columns_ref[at:at + LANES, :] = strength[:, at:at + LANES].T.astype(BF16)
+    for board in range(0, boards, 2):
+        lane = lax.broadcasted_iota(jnp.int32, (boards, 2 * LANES), 1) // LANES + board
+        pick = (lane == lax.broadcasted_iota(jnp.int32, lane.shape, 0)).astype(BF16)
+        both = jnp.dot(columns_ref[...], pick, preferred_element_type=F32).astype(BF16)
+        wide_ref[board] = both[:, :LANES]
+        wide_ref[board + 1] = both[:, LANES:]
 
     def clear_of(card):
         return jnp.where((lower == card) | (upper == card), 0.0, 1.0)
@@ -124,17 +128,14 @@
         for chunk in range(0, width, DEPTH):
             stop = min(chunk + DEPTH, width)
             for down in range(chunk, stop, 32):
-                column = [
-                    jnp.broadcast_to(columns_ref[at_group, down:down + 32, i:i + 1], (32, LANES)).astype(BF16)
-                    for i in range(group)
-                ]
+                column = [wide_ref[first + i, down:down + 32, :] for i in range(group)]
                 for at in range(0, width, LANES):
                     free = free_ref[down:down + 32, at:at + LANES]
-                    minus = minus_ref[down:down + 32, at:at + LANES]
                     for i in range(group):
                         row = rows_ref[first + i, :, at:at + LANES]
                         gap = jnp.concatenate([row, row], axis=0) - column[i]
-                        payoff_ref[i, down:down + 32, at:at + LANES] = jnp.minimum(jnp.maximum(gap, minus), free).astype(F8)
+                        sign = jnp.minimum(jnp.maximum(gap, -1.0), 1.0) * free
+                        payoff_ref[i, down:down + 32, at:at + LANES] = sign.astype(F8)
             for i in range(group):
                 product = jnp.dot(lines[i][:, chunk:stop], payoff_ref[i, chunk:stop, :], preferred_element_type=F32)
                 if chunk == 0:
@@ -166,12 +167,12 @@
         functools.partial(board_kernel, hands=hands),
         in_specs=[pl.BlockSpec(memory_space=pl.ANY)] * len(args),
         out_specs=pl.BlockSpec(memory_space=pltpu.VMEM),
-        out_shape=jax.ShapeDtypeStruct((flops, hands), F32),
+        out_shape=pltpu.VMEM((flops, hands), F32),
         scratch_shapes=held + [
             pltpu.VMEM((width, width), BF16),
-            pltpu.VMEM((width, width), BF16),
             pltpu.VMEM((boards, 16, width), BF16),
-            pltpu.VMEM((boards // GROUP, width, GROUP), F32),
+            pltpu.VMEM((width, boards), BF16),
+            pltpu.VMEM((boards, width, LANES), BF16),
             pltpu.VMEM((flops, 1, width), F32),
             pltpu.VMEM((flops, 4, width), F32),
             pltpu.VMEM((GROUP, width, width), F8),
@@ -184,8 +185,9 @@
     )(*args)
 
 
-def swap(values, axis, size, flip, combine):
-    return combine(values, lax.ppermute(values, axis, [(i, i ^ flip) for i in range(size)]))
+def swaps(values, axis, size, flips, combine):
+    parts = [lax.ppermute(values, axis, [(i, i ^ flip) for i in range(size)]) for flip in flips]
+    return functools.reduce(combine, parts, values)
 
 
 def local(flop_cards, turn_cards, river_cards, ranks, flop_reach, turn_policy, river_policy, stake):
@@ -193,14 +195,13 @@
         flop_cards, turn_cards[:, 0], river_cards[:, 0], ranks[:, 0], flop_reach, turn_policy[:, 0, 0],
         river_policy[:, 0, :, 0], stake[0]
     )
-    values = swap(values, "z_lo", 2, 1, jnp.maximum)
-    values = swap(values, "y", 4, 1, jnp.maximum)
-    values = swap(values, "y", 4, 3, jnp.maximum)
-    total = swap(values, "core", 2, 1, jnp.add)
-    total = swap(total, "x", 4, 1, jnp.add)
-    total = swap(total, "x", 4, 3, jnp.add)
-    total = swap(total, "z_hi", 4, 1, jnp.add)
-    total = swap(total, "z_hi", 4, 3, jnp.add)
+    line = ("z_lo", "y")
+    copies = jnp.broadcast_to(values[None], (lax.axis_size(line),) + values.shape)
+    values = jnp.max(lax.all_to_all(copies, line, 0, 0), axis=0)
+    total = swaps(values, "core", 2, (1,), jnp.add)
+    total = swaps(total, "x", 4, (1, 3, 2), jnp.add)
+    total = swaps(total, "z_hi", 4, (1,), jnp.add)
+    total = swaps(total, "z_hi", 4, (3,), jnp.add)
     return values[:, None, :], total / 32
 
 

time: 51.3 us -> 47.1 us (0.918)
  blocking collectives: 0 us -> 12 us
  waiting for transfers between devices: 15.4 us -> 7.57 us
  starting transfers between devices: 19.3 us -> 12.2 us
  other arithmetic: 1.36 us -> 0.67 us
    all_to_all x0 -> x1, blocking collectives: none -> 12 us  [local(): values = jnp.max(lax.all_to_all(copies, line, 0, 0), axis=0)]
    ppermute x8 -> x6, waiting for transfers between devices: 15.4 us -> 7.57 us  [swaps(): lax.ppermute(values, axis, [(i, i ^ flip) for i in range(size)])]
    ppermute x8 -> x6, starting transfers between devices: 19.3 us -> 12.2 us  [swaps(): lax.ppermute(values, axis, [(i, i ^ flip) for i in range(size)])]
    max x3 -> x0, other arithmetic: 0.73 us -> none  [swap(): combine(values, lax.ppermute(values, axis, [(i, i ^ flip) for i in range(...]
    pallas_call x1, Pallas kernels: 13.7 us -> 13.2 us  [board_values(): pl.pallas_call(functools.partial(board_kernel, hands=hands), in_specs=[pl...]
  transfers between devices with their start and end apart: 8 -> 6, of which waited for: 8 -> 6; matrix products, arithmetic and copies ran while one was open for 1% -> 1% of each run, Pallas kernels for 0% -> 0%
where the time goes in v3:
time: 47.1 us; the launch traced here: 46.9 us
  Pallas kernels  13.2 us (28%)
  starting transfers between devices  12.2 us (26%)
  blocking collectives  12 us (25%)
  waiting for transfers between devices  7.57 us (16%)
  other arithmetic  0.67 us (1%)
  between operations  0.67 us (1%)
  local copies, waits for them, and re-layouts  0.64 us (1%)
    pallas_call x1, Pallas kernels, board_values(): pl.pallas_call(functools.partial(board_kernel, hands=hands), in_specs=[pl...  13.2 us
    ppermute x6, starting transfers between devices, swaps(): lax.ppermute(values, axis, [(i, i ^ flip) for i in range(size)])  12.2 us
    all_to_all x1, blocking collectives, local(): values = jnp.max(lax.all_to_all(copies, line, 0, 0), axis=0)  12 us
    ppermute x6, waiting for transfers between devices, swaps(): lax.ppermute(values, axis, [(i, i ^ flip) for i in range(size)])  7.57 us
  transfers between devices with their start and end apart: 6, of which 6 were waited for; matrix products, arithmetic and copies ran while one was open for 1% of the time, Pallas kernels for 0%

profile of v3, /device:TPU:6, one launch (start us, length us, event | category | flops | bytes accessed | tf_op | source)
XLA Modules:
  0.0 46.9 jit_solution(2769751130269891124)
XLA Ops:
  0.6 13.2 %boards.1 = f32[2,1326]{1,0:T(2,128)S(1)} custom-call(s32[2,3]{1,0:T(2,128)} %flop_cards_in.1, s32[2]{0:T(128)} %bitcast.13, s32[2,8]{1,0:T(2,128)} %bitcast.12, s32[16,1326]{1,0:T(8,128)} %bitcast.9, f32[2,1326]{1,0:T(2,128)} %flop_reach_in.1, bf16[2,4,1326]{2,1,0:T(4,128)(2,1)} %bitcast.10, f32[4,4,4]{2,1,0:T(4,128)} %bitcast.11, ...), custom_call_target="tpu_custom_call" | custom-call | tf_op jit(solution)/shard_map/boards/pallas_call | solution.py:166
  13.9 12.0 %all_to_all.5 = f32[8,2,1326]{2,1,0:T(2,128)S(1)} all-to-all(f32[8,2,1326]{2,1,0:T(2,128)S(1)} %broadcast_in_dim.4), channel_id=1, replica_groups=mesh['z_hi'=4,'x'=4,'core'=2,'z_lo'=2,'y'=4] {'z_lo','y'}, dimensions={0} | all-to-all | bytes 169728 | tf_op jit(solution)/shard_map/all_to_all | solution.py:200
  25.9 0.1 collective-permute-start
  26.0 1.2 %collective-permute-done = f32[2,1326]{1,0:T(2,128)S(1)} collective-permute-done((f32[2,1326]{1,0:T(2,128)S(1)}, f32[2,1326]{1,0:T(2,128)S(1)}, u32[]{:S(2)}, u32[]{:S(2)}) %collective-permute-start) | collective-permute-done | bytes 10640 | tf_op jit(solution)/shard_map/ppermute | solution.py:189
  27.2 1.5 %collective-permute-start.3 = (f32[2,1326]{1,0:T(2,128)S(1)}, f32[2,1326]{1,0:T(2,128)S(1)}, u32[]{:S(2)}, u32[]{:S(2)}) collective-permute-start(f32[2,1326]{1,0:T(2,128)S(1)} %add.18), channel_id=1, source_target_pairs={{0,32},{16,48},{32,0},{48,16},{1,33},{17,49},{33,1},{49,17},{2,34}... | collective-permute-start | bytes 31832 | tf_op jit(solution)/shard_map/ppermute | solution.py:189
  28.7 2.1 %collective-permute-start.2 = (f32[2,1326]{1,0:T(2,128)S(1)}, f32[2,1326]{1,0:T(2,128)S(1)}, u32[]{:S(2)}, u32[]{:S(2)}) collective-permute-start(f32[2,1326]{1,0:T(2,128)S(1)} %add.18), channel_id=1, source_target_pairs={{0,48},{16,32},{32,16},{48,0},{1,49},{17,33},{33,17},{49,1},{2,50}... | collective-permute-start | bytes 31832 | tf_op jit(solution)/shard_map/ppermute | solution.py:189
  30.8 0.0 collective-permute-start.1
  30.8 1.8 %collective-permute-done.3 = f32[2,1326]{1,0:T(2,128)S(1)} collective-permute-done((f32[2,1326]{1,0:T(2,128)S(1)}, f32[2,1326]{1,0:T(2,128)S(1)}, u32[]{:S(2)}, u32[]{:S(2)}) %collective-permute-start.3) | collective-permute-done | bytes 10640 | tf_op jit(solution)/shard_map/ppermute | solution.py:189
  32.6 1.0 %collective-permute-done.2 = f32[2,1326]{1,0:T(2,128)S(1)} collective-permute-done((f32[2,1326]{1,0:T(2,128)S(1)}, f32[2,1326]{1,0:T(2,128)S(1)}, u32[]{:S(2)}, u32[]{:S(2)}) %collective-permute-start.2) | collective-permute-done | bytes 10640 | tf_op jit(solution)/shard_map/ppermute | solution.py:189
  33.6 0.9 %collective-permute-done.1 = f32[2,1326]{1,0:T(2,128)S(1)} collective-permute-done((f32[2,1326]{1,0:T(2,128)S(1)}, f32[2,1326]{1,0:T(2,128)S(1)}, u32[]{:S(2)}, u32[]{:S(2)}) %collective-permute-start.1) | collective-permute-done | bytes 10640 | tf_op jit(solution)/shard_map/ppermute | solution.py:189
  34.5 3.4 %collective-permute-start.4 = (f32[2,1326]{1,0:T(2,128)S(1)}, f32[2,1326]{1,0:T(2,128)S(1)}, u32[]{:S(2)}, u32[]{:S(2)}) collective-permute-start(f32[2,1326]{1,0:T(2,128)S(1)} %add_add_fusion), channel_id=1, source_target_pairs={{0,64},{64,0},{128,192},{192,128},{1,65},{65,1},{129,193},{193,129... | collective-permute-start | bytes 31832 | tf_op jit(solution)/shard_map/ppermute | solution.py:189
  37.9 1.7 %collective-permute-done.4 = f32[2,1326]{1,0:T(2,128)S(1)} collective-permute-done((f32[2,1326]{1,0:T(2,128)S(1)}, f32[2,1326]{1,0:T(2,128)S(1)}, u32[]{:S(2)}, u32[]{:S(2)}) %collective-permute-start.4) | collective-permute-done | bytes 10640 | tf_op jit(solution)/shard_map/ppermute | solution.py:189
  39.5 5.1 %collective-permute-start.5 = (f32[2,1326]{1,0:T(2,128)S(1)}, f32[2,1326]{1,0:T(2,128)S(1)}, u32[]{:S(2)}, u32[]{:S(2)}) collective-permute-start(f32[2,1326]{1,0:T(2,128)S(1)} %add.22), channel_id=1, source_target_pairs={{0,192},{64,128},{128,64},{192,0},{1,193},{65,129},{129,65},{193,1... | collective-permute-start | bytes 31832 | tf_op jit(solution)/shard_map/ppermute | solution.py:189
  44.7 0.6 %copy.12 = f32[2,1,1326]{2,1,0:T(1,128)} copy(f32[2,1,1326]{2,0,1:T(2,128)S(1)} %bitcast.8) | data formatting | bytes 21216
  45.3 1.1 %collective-permute-done.5 = f32[2,1326]{1,0:T(2,128)S(1)} collective-permute-done((f32[2,1326]{1,0:T(2,128)S(1)}, f32[2,1326]{1,0:T(2,128)S(1)}, u32[]{:S(2)}, u32[]{:S(2)}) %collective-permute-start.5) | collective-permute-done | bytes 10640 | tf_op jit(solution)/shard_map/ppermute | solution.py:189
  46.3 0.6 %add_multiply_fusion = f32[2,1326]{1,0:T(2,128)} fusion(f32[2,1326]{1,0:T(2,128)S(1)} %add.22, f32[2,1326]{1,0:T(2,128)S(1)} %collective-permute-done.5), kind=kLoop, calls=%fused_computation | loop fusion | flops 5304 | bytes 31824 | tf_op jit(solution)/shard_map/div | solution.py:205
  (5 shorter events, 0.1 us)
Async XLA Ops:
  25.9 1.3 %collective-permute-start = (f32[2,1326]{1,0:T(2,128)S(1)}, f32[2,1326]{1,0:T(2,128)S(1)}, u32[]{:S(2)}, u32[]{:S(2)}) collective-permute-start(f32[2,1326]{1,0:T(2,128)S(1)} %reduce_max.9), channel_id=1, source_target_pairs={{0,8},{8,0},{1,9},{9,1},{2,10},{10,2},{3,11},{11,3},{4,12},{12,4},... | collective-permute-start | bytes 31832 | tf_op jit(solution)/shard_map/ppermute | solution.py:189
  27.2 5.3 %collective-permute-start.3 = (f32[2,1326]{1,0:T(2,128)S(1)}, f32[2,1326]{1,0:T(2,128)S(1)}, u32[]{:S(2)}, u32[]{:S(2)}) collective-permute-start(f32[2,1326]{1,0:T(2,128)S(1)} %add.18), channel_id=1, source_target_pairs={{0,32},{16,48},{32,0},{48,16},{1,33},{17,49},{33,1},{49,17},{2,34}... | collective-permute-start | bytes 31832 | tf_op jit(solution)/shard_map/ppermute | solution.py:189
  28.7 4.9 %collective-permute-start.2 = (f32[2,1326]{1,0:T(2,128)S(1)}, f32[2,1326]{1,0:T(2,128)S(1)}, u32[]{:S(2)}, u32[]{:S(2)}) collective-permute-start(f32[2,1326]{1,0:T(2,128)S(1)} %add.18), channel_id=1, source_target_pairs={{0,48},{16,32},{32,16},{48,0},{1,49},{17,33},{33,17},{49,1},{2,50}... | collective-permute-start | bytes 31832 | tf_op jit(solution)/shard_map/ppermute | solution.py:189
  30.8 3.7 %collective-permute-start.1 = (f32[2,1326]{1,0:T(2,128)S(1)}, f32[2,1326]{1,0:T(2,128)S(1)}, u32[]{:S(2)}, u32[]{:S(2)}) collective-permute-start(f32[2,1326]{1,0:T(2,128)S(1)} %add.18), channel_id=1, source_target_pairs={{0,16},{16,0},{32,48},{48,32},{1,17},{17,1},{33,49},{49,33},{2,18}... | collective-permute-start | bytes 31832 | tf_op jit(solution)/shard_map/ppermute | solution.py:189
  34.5 5.0 %collective-permute-start.4 = (f32[2,1326]{1,0:T(2,128)S(1)}, f32[2,1326]{1,0:T(2,128)S(1)}, u32[]{:S(2)}, u32[]{:S(2)}) collective-permute-start(f32[2,1326]{1,0:T(2,128)S(1)} %add_add_fusion), channel_id=1, source_target_pairs={{0,64},{64,0},{128,192},{192,128},{1,65},{65,1},{129,193},{193,129... | collective-permute-start | bytes 31832 | tf_op jit(solution)/shard_map/ppermute | solution.py:189
  39.5 6.8 %collective-permute-start.5 = (f32[2,1326]{1,0:T(2,128)S(1)}, f32[2,1326]{1,0:T(2,128)S(1)}, u32[]{:S(2)}, u32[]{:S(2)}) collective-permute-start(f32[2,1326]{1,0:T(2,128)S(1)} %add.22), channel_id=1, source_target_pairs={{0,192},{64,128},{128,64},{192,0},{1,193},{65,129},{129,65},{193,1... | collective-permute-start | bytes 31832 | tf_op jit(solution)/shard_map/ppermute | solution.py:189

commit v4 on v3

--- a/solution.py
+++ b/solution.py
@@ -15,6 +15,7 @@
 BF16 = jnp.bfloat16
 GROUP = 4
 DEPTH = 256
+SPLIT = 8
 
 
 def padded(hands):
@@ -49,6 +50,7 @@
     flops, rivers = river_cards.shape
     boards = flops * rivers
     width = padded(hands)
+    depth = -(-hands // 64) * 64
     group = GROUP
     tiles = [(at, min(256, width - at)) for at in range(0, width, 256)]
     pairs = [
@@ -80,12 +82,17 @@
         rows_ref[row] = jnp.broadcast_to(strength[row:row + 1], (16, width)).astype(BF16)
     for at in range(0, width, LANES):
         columns_ref[at:at + LANES, :] = strength[:, at:at + LANES].T.astype(BF16)
-    for board in range(0, boards, 2):
+    half = SPLIT
+    for board in range(half, boards):
+        for down in range(0, depth, 64):
+            column = columns_ref[down:down + 64, board:board + 1].astype(F32)
+            wide_ref[board, down:down + 64, :] = jnp.broadcast_to(column, (64, LANES)).astype(BF16)
+    for board in range(0, half, 2):
         lane = lax.broadcasted_iota(jnp.int32, (boards, 2 * LANES), 1) // LANES + board
         pick = (lane == lax.broadcasted_iota(jnp.int32, lane.shape, 0)).astype(BF16)
-        both = jnp.dot(columns_ref[...], pick, preferred_element_type=F32).astype(BF16)
-        wide_ref[board] = both[:, :LANES]
-        wide_ref[board + 1] = both[:, LANES:]
+        both = jnp.dot(columns_ref[:depth, :], pick, preferred_element_type=F32).astype(BF16)
+        wide_ref[board, :depth] = both[:, :LANES]
+        wide_ref[board + 1, :depth] = both[:, LANES:]
 
     def clear_of(card):
         return jnp.where((lower == card) | (upper == card), 0.0, 1.0)
@@ -125,8 +132,8 @@
             reach = share.reshape(4, 4, hands) * (entry_ref[flop] * clear)[:, None, :hands]
             lines.append(widen(reach.reshape(16, hands)).astype(BF16))
             clears.append(clear)
-        for chunk in range(0, width, DEPTH):
-            stop = min(chunk + DEPTH, width)
+        for chunk in range(0, depth, DEPTH):
+            stop = min(chunk + DEPTH, depth)
             for down in range(chunk, stop, 32):
                 column = [wide_ref[first + i, down:down + 32, :] for i in range(group)]
                 for at in range(0, width, LANES):
@@ -199,7 +206,9 @@
     copies = jnp.broadcast_to(values[None], (lax.axis_size(line),) + values.shape)
     values = jnp.max(lax.all_to_all(copies, line, 0, 0), axis=0)
     total = swaps(values, "core", 2, (1,), jnp.add)
-    total = swaps(total, "x", 4, (1, 3, 2), jnp.add)
+    pairs = [(2 * i + core, 2 * (i ^ flip) + core) for i in range(4) for core, flip in ((0, 1), (1, 3))]
+    near = lax.ppermute(total, ("x", "core"), pairs)
+    total = swaps(total, "x", 4, (2,), jnp.add) + near + lax.ppermute(near, "core", [(0, 1), (1, 0)])
     total = swaps(total, "z_hi", 4, (1,), jnp.add)
     total = swaps(total, "z_hi", 4, (3,), jnp.add)
     return values[:, None, :], total / 32

time: 47.1 us -> 45.4 us (0.964)
  starting transfers between devices: 12.2 us -> 10.7 us
  Pallas kernels: 13.2 us -> 12.4 us
    ppermute x6 -> x4, starting transfers between devices: 12.2 us -> 9.68 us  [swaps(): lax.ppermute(values, axis, [(i, i ^ flip) for i in range(size)])]
    ppermute x0 -> x2, waiting for transfers between devices: none -> 1.74 us  [the longest x1 1.74 us: local(): near = lax.ppermute(total, ('x', 'core'), pairs)]
    ppermute x6 -> x4, waiting for transfers between devices: 7.57 us -> 6.08 us  [swaps(): lax.ppermute(values, axis, [(i, i ^ flip) for i in range(size)])]
    ppermute x0 -> x2, starting transfers between devices: none -> 1.06 us  [the longest x1 0.92 us: local(): near = lax.ppermute(total, ('x', 'core'), pairs)]
    pallas_call x1, Pallas kernels: 13.2 us -> 12.4 us  [board_values(): pl.pallas_call(functools.partial(board_kernel, hands=hands), in_specs=[pl...]
  transfers between devices with their start and end apart: 6 -> 6, of which waited for: 6 -> 5; matrix products, arithmetic and copies ran while one was open for 1% -> 1% of each run, Pallas kernels for 0% -> 0%
where the time goes in v4:
time: 45.4 us; the launch traced here: 44.9 us
  Pallas kernels  12.4 us (27%)
  blocking collectives  12 us (26%)
  starting transfers between devices  10.7 us (24%)
  waiting for transfers between devices  7.83 us (17%)
  other arithmetic  0.67 us (1%)
  between operations  0.67 us (1%)
  local copies, waits for them, and re-layouts  0.64 us (1%)
    pallas_call x1, Pallas kernels, board_values(): pl.pallas_call(functools.partial(board_kernel, hands=hands), in_specs=[pl...  12.4 us
    all_to_all x1, blocking collectives, local(): values = jnp.max(lax.all_to_all(copies, line, 0, 0), axis=0)  12 us
    ppermute x4, starting transfers between devices, swaps(): lax.ppermute(values, axis, [(i, i ^ flip) for i in range(size)])  9.68 us
    ppermute x4, waiting for transfers between devices, swaps(): lax.ppermute(values, axis, [(i, i ^ flip) for i in range(size)])  6.08 us
    ppermute x1, waiting for transfers between devices, local(): near = lax.ppermute(total, ('x', 'core'), pairs)  1.74 us
    ppermute x1, starting transfers between devices, local(): near = lax.ppermute(total, ('x', 'core'), pairs)  0.92 us
  transfers between devices with their start and end apart: 6, of which 5 were waited for; matrix products, arithmetic and copies ran while one was open for 1% of the time, Pallas kernels for 0%

profile of v4, /device:TPU:6, one launch (start us, length us, event | category | flops | bytes accessed | tf_op | source)
XLA Modules:
  0.0 44.9 jit_solution(16469762826627930017)
XLA Ops:
  0.6 12.4 %boards.1 = f32[2,1326]{1,0:T(2,128)S(1)} custom-call(s32[2,3]{1,0:T(2,128)} %flop_cards_in.1, s32[2]{0:T(128)} %bitcast.13, s32[2,8]{1,0:T(2,128)} %bitcast.12, s32[16,1326]{1,0:T(8,128)} %bitcast.9, f32[2,1326]{1,0:T(2,128)} %flop_reach_in.1, bf16[2,4,1326]{2,1,0:T(4,128)(2,1)} %bitcast.10, f32[4,4,4]{2,1,0:T(4,128)} %bitcast.11, ...), custom_call_target="tpu_custom_call" | custom-call | tf_op jit(solution)/shard_map/boards/pallas_call | solution.py:173
  13.0 12.0 %all_to_all.5 = f32[8,2,1326]{2,1,0:T(2,128)S(1)} all-to-all(f32[8,2,1326]{2,1,0:T(2,128)S(1)} %broadcast_in_dim.4), channel_id=1, replica_groups=mesh['z_hi'=4,'x'=4,'core'=2,'z_lo'=2,'y'=4] {'z_lo','y'}, dimensions={0} | all-to-all | bytes 169728 | tf_op jit(solution)/shard_map/all_to_all | solution.py:207
  25.1 0.1 collective-permute-start
  25.2 1.2 %collective-permute-done = f32[2,1326]{1,0:T(2,128)S(1)} collective-permute-done((f32[2,1326]{1,0:T(2,128)S(1)}, f32[2,1326]{1,0:T(2,128)S(1)}, u32[]{:S(2)}, u32[]{:S(2)}) %collective-permute-start) | collective-permute-done | bytes 10640 | tf_op jit(solution)/shard_map/ppermute | solution.py:196
  26.4 0.9 %collective-permute-start.2 = (f32[2,1326]{1,0:T(2,128)S(1)}, f32[2,1326]{1,0:T(2,128)S(1)}, u32[]{:S(2)}, u32[]{:S(2)}) collective-permute-start(f32[2,1326]{1,0:T(2,128)S(1)} %add.18), channel_id=1, source_target_pairs={{0,16},{8,56},{16,0},{24,40},{32,48},{40,24},{48,32},{56,8},{1,17}... | collective-permute-start | bytes 31832 | tf_op jit(solution)/shard_map/ppermute | solution.py:210
  27.3 1.1 %collective-permute-start.1 = (f32[2,1326]{1,0:T(2,128)S(1)}, f32[2,1326]{1,0:T(2,128)S(1)}, u32[]{:S(2)}, u32[]{:S(2)}) collective-permute-start(f32[2,1326]{1,0:T(2,128)S(1)} %add.18), channel_id=1, source_target_pairs={{0,32},{16,48},{32,0},{48,16},{1,33},{17,49},{33,1},{49,17},{2,34}... | collective-permute-start | bytes 31832 | tf_op jit(solution)/shard_map/ppermute | solution.py:196
  28.4 1.7 %collective-permute-done.2 = f32[2,1326]{1,0:T(2,128)S(1)} collective-permute-done((f32[2,1326]{1,0:T(2,128)S(1)}, f32[2,1326]{1,0:T(2,128)S(1)}, u32[]{:S(2)}, u32[]{:S(2)}) %collective-permute-start.2) | collective-permute-done | bytes 10640 | tf_op jit(solution)/shard_map/ppermute | solution.py:210
  30.1 0.1 collective-permute-start.3
  30.3 2.2 %collective-permute-done.1 = f32[2,1326]{1,0:T(2,128)S(1)} collective-permute-done((f32[2,1326]{1,0:T(2,128)S(1)}, f32[2,1326]{1,0:T(2,128)S(1)}, u32[]{:S(2)}, u32[]{:S(2)}) %collective-permute-start.1) | collective-permute-done | bytes 10640 | tf_op jit(solution)/shard_map/ppermute | solution.py:196
  32.5 0.0 collective-permute-done.3
  32.5 3.4 %collective-permute-start.4 = (f32[2,1326]{1,0:T(2,128)S(1)}, f32[2,1326]{1,0:T(2,128)S(1)}, u32[]{:S(2)}, u32[]{:S(2)}) collective-permute-start(f32[2,1326]{1,0:T(2,128)S(1)} %add_add_fusion), channel_id=1, source_target_pairs={{0,64},{64,0},{128,192},{192,128},{1,65},{65,1},{129,193},{193,129... | collective-permute-start | bytes 31832 | tf_op jit(solution)/shard_map/ppermute | solution.py:196
  35.9 1.7 %collective-permute-done.4 = f32[2,1326]{1,0:T(2,128)S(1)} collective-permute-done((f32[2,1326]{1,0:T(2,128)S(1)}, f32[2,1326]{1,0:T(2,128)S(1)}, u32[]{:S(2)}, u32[]{:S(2)}) %collective-permute-start.4) | collective-permute-done | bytes 10640 | tf_op jit(solution)/shard_map/ppermute | solution.py:196
  37.5 5.1 %collective-permute-start.5 = (f32[2,1326]{1,0:T(2,128)S(1)}, f32[2,1326]{1,0:T(2,128)S(1)}, u32[]{:S(2)}, u32[]{:S(2)}) collective-permute-start(f32[2,1326]{1,0:T(2,128)S(1)} %add.22), channel_id=1, source_target_pairs={{0,192},{64,128},{128,64},{192,0},{1,193},{65,129},{129,65},{193,1... | collective-permute-start | bytes 31832 | tf_op jit(solution)/shard_map/ppermute | solution.py:196
  42.7 0.6 %copy.12 = f32[2,1,1326]{2,1,0:T(1,128)} copy(f32[2,1,1326]{2,0,1:T(2,128)S(1)} %bitcast.8) | data formatting | bytes 21216
  43.3 1.1 %collective-permute-done.5 = f32[2,1326]{1,0:T(2,128)S(1)} collective-permute-done((f32[2,1326]{1,0:T(2,128)S(1)}, f32[2,1326]{1,0:T(2,128)S(1)}, u32[]{:S(2)}, u32[]{:S(2)}) %collective-permute-start.5) | collective-permute-done | bytes 10640 | tf_op jit(solution)/shard_map/ppermute | solution.py:196
  44.3 0.6 %add_multiply_fusion = f32[2,1326]{1,0:T(2,128)} fusion(f32[2,1326]{1,0:T(2,128)S(1)} %add.22, f32[2,1326]{1,0:T(2,128)S(1)} %collective-permute-done.5), kind=kLoop, calls=%fused_computation | loop fusion | flops 5304 | bytes 31824 | tf_op jit(solution)/shard_map/div | solution.py:214
  (5 shorter events, 0.1 us)
Async XLA Ops:
  25.1 1.3 %collective-permute-start = (f32[2,1326]{1,0:T(2,128)S(1)}, f32[2,1326]{1,0:T(2,128)S(1)}, u32[]{:S(2)}, u32[]{:S(2)}) collective-permute-start(f32[2,1326]{1,0:T(2,128)S(1)} %reduce_max.9), channel_id=1, source_target_pairs={{0,8},{8,0},{1,9},{9,1},{2,10},{10,2},{3,11},{11,3},{4,12},{12,4},... | collective-permute-start | bytes 31832 | tf_op jit(solution)/shard_map/ppermute | solution.py:196
  26.4 3.8 %collective-permute-start.2 = (f32[2,1326]{1,0:T(2,128)S(1)}, f32[2,1326]{1,0:T(2,128)S(1)}, u32[]{:S(2)}, u32[]{:S(2)}) collective-permute-start(f32[2,1326]{1,0:T(2,128)S(1)} %add.18), channel_id=1, source_target_pairs={{0,16},{8,56},{16,0},{24,40},{32,48},{40,24},{48,32},{56,8},{1,17}... | collective-permute-start | bytes 31832 | tf_op jit(solution)/shard_map/ppermute | solution.py:210
  27.3 5.2 %collective-permute-start.1 = (f32[2,1326]{1,0:T(2,128)S(1)}, f32[2,1326]{1,0:T(2,128)S(1)}, u32[]{:S(2)}, u32[]{:S(2)}) collective-permute-start(f32[2,1326]{1,0:T(2,128)S(1)} %add.18), channel_id=1, source_target_pairs={{0,32},{16,48},{32,0},{48,16},{1,33},{17,49},{33,1},{49,17},{2,34}... | collective-permute-start | bytes 31832 | tf_op jit(solution)/shard_map/ppermute | solution.py:196
  30.1 2.3 %collective-permute-start.3 = (f32[2,1326]{1,0:T(2,128)S(1)}, f32[2,1326]{1,0:T(2,128)S(1)}, u32[]{:S(2)}, u32[]{:S(2)}) collective-permute-start(f32[2,1326]{1,0:T(2,128)S(1)} %collective-permute-done.2), channel_id=1, source_target_pairs={{0,8},{8,0},{1,9},{9,1},{2,10},{10,2},{3,11},{11,3},{4,12},{12,4},... | collective-permute-start | bytes 31832 | tf_op jit(solution)/shard_map/ppermute | solution.py:211
  32.5 5.0 %collective-permute-start.4 = (f32[2,1326]{1,0:T(2,128)S(1)}, f32[2,1326]{1,0:T(2,128)S(1)}, u32[]{:S(2)}, u32[]{:S(2)}) collective-permute-start(f32[2,1326]{1,0:T(2,128)S(1)} %add_add_fusion), channel_id=1, source_target_pairs={{0,64},{64,0},{128,192},{192,128},{1,65},{65,1},{129,193},{193,129... | collective-permute-start | bytes 31832 | tf_op jit(solution)/shard_map/ppermute | solution.py:196
  37.5 6.8 %collective-permute-start.5 = (f32[2,1326]{1,0:T(2,128)S(1)}, f32[2,1326]{1,0:T(2,128)S(1)}, u32[]{:S(2)}, u32[]{:S(2)}) collective-permute-start(f32[2,1326]{1,0:T(2,128)S(1)} %add.22), channel_id=1, source_target_pairs={{0,192},{64,128},{128,64},{192,0},{1,193},{65,129},{129,65},{193,1... | collective-permute-start | bytes 31832 | tf_op jit(solution)/shard_map/ppermute | solution.py:196

commit v5 on v4

--- a/solution.py
+++ b/solution.py
@@ -16,6 +16,7 @@
 GROUP = 4
 DEPTH = 256
 SPLIT = 8
+COPIES = 16
 
 
 def padded(hands):
@@ -58,8 +59,8 @@
         (flop_reach_in, flop_reach_ref), (turn_in, turn_ref), (stake_in, stake_ref),
     ]
     copies = [pltpu.make_async_copy(source, target, sems.at[i]) for i, (source, target) in enumerate(pairs)]
-    for copy in copies:
-        copy.start()
+    for i in (3, 5, 4, 6, 0, 1, 2):
+        copies[i].start()
 
     def river_copy(board):
         return pltpu.make_async_copy(river_in.at[board], river_ref.at[board], river_sems.at[board])
@@ -74,8 +75,7 @@
         shared = lax.dot_general(holds, holds[:, at:at + size], (((0,), (0,)), ((), ())), preferred_element_type=F32)
         free = jnp.maximum(1.0 - shared, 0.0).astype(BF16)
         free_ref[:, at:at + size] = free
-    for copy in copies:
-        copy.wait()
+    copies[3].wait()
     strength = ordered(ranks_ref[...])
     strength = jnp.concatenate([strength, jnp.zeros((boards, width - hands), F32)], axis=1)
     for row in range(boards):
@@ -93,6 +93,9 @@
         both = jnp.dot(columns_ref[:depth, :], pick, preferred_element_type=F32).astype(BF16)
         wide_ref[board, :depth] = both[:, :LANES]
         wide_ref[board + 1, :depth] = both[:, LANES:]
+
+    for i in (0, 1, 2, 4, 5, 6):
+        copies[i].wait()
 
     def clear_of(card):
         return jnp.where((lower == card) | (upper == card), 0.0, 1.0)
@@ -158,7 +161,9 @@
     groups = rivers // group
     for flop in range(flops):
         value = lax.fori_loop(flop * groups, (flop + 1) * groups, one_group, jnp.zeros((1, width), F32))
-        out_ref[flop:flop + 1, :] = (value * clear_ref[flop] * (1 / rivers))[:, :hands]
+        result = (value * clear_ref[flop] * (1 / rivers))[:, :hands]
+        for i in range(out_ref.shape[0]):
+            out_ref[i, flop:flop + 1, :] = result
 
 
 def board_values(flop_cards, turn_cards, river_cards, ranks, flop_reach, turn_policy, river_policy, stake):
@@ -174,7 +179,7 @@
         functools.partial(board_kernel, hands=hands),
         in_specs=[pl.BlockSpec(memory_space=pl.ANY)] * len(args),
         out_specs=pl.BlockSpec(memory_space=pltpu.VMEM),
-        out_shape=pltpu.VMEM((flops, hands), F32),
+        out_shape=pltpu.VMEM((COPIES, flops, hands), F32),
         scratch_shapes=held + [
             pltpu.VMEM((width, width), BF16),
             pltpu.VMEM((boards, 16, width), BF16),
@@ -198,14 +203,15 @@
 
 
 def local(flop_cards, turn_cards, river_cards, ranks, flop_reach, turn_policy, river_policy, stake):
-    values = board_values(
+    copies = board_values(
         flop_cards, turn_cards[:, 0], river_cards[:, 0], ranks[:, 0], flop_reach, turn_policy[:, 0, 0],
         river_policy[:, 0, :, 0], stake[0]
     )
-    line = ("z_lo", "y")
-    copies = jnp.broadcast_to(values[None], (lax.axis_size(line),) + values.shape)
-    values = jnp.max(lax.all_to_all(copies, line, 0, 0), axis=0)
-    total = swaps(values, "core", 2, (1,), jnp.add)
+    group = ("core", "z_lo", "y")
+    gathered = lax.all_to_all(copies, group, 0, 0).reshape(2, -1, *copies.shape[1:])
+    first, second = jnp.max(gathered[0], axis=0), jnp.max(gathered[1], axis=0)
+    values = jnp.where(lax.axis_index("core") == 0, first, second)
+    total = first + second
     pairs = [(2 * i + core, 2 * (i ^ flip) + core) for i in range(4) for core, flip in ((0, 1), (1, 3))]
     near = lax.ppermute(total, ("x", "core"), pairs)
     total = swaps(total, "x", 4, (2,), jnp.add) + near + lax.ppermute(near, "core", [(0, 1), (1, 0)])

time: 45.4 us -> 45.7 us (level)
  blocking collectives: 12 us -> 0 us
  starting transfers between devices: 10.7 us -> 16.8 us
  waiting for transfers between devices: 7.83 us -> 13.5 us
  Pallas kernels: 12.4 us -> 12.9 us
    all_to_all x1 -> x0, blocking collectives: 12 us -> none  [local(): values = jnp.max(lax.all_to_all(copies, line, 0, 0), axis=0)]
    all_to_all x0 -> x1, waiting for transfers between devices: none -> 7.01 us  [local(): lax.all_to_all(copies, group, 0, 0).reshape(2, -1, *copies.shape[1:])]
    all_to_all x0 -> x1, starting transfers between devices: none -> 5.95 us  [local(): lax.all_to_all(copies, group, 0, 0).reshape(2, -1, *copies.shape[1:])]
    ppermute x4 -> x3, waiting for transfers between devices: 6.08 us -> 4.73 us  [swaps(): lax.ppermute(values, axis, [(i, i ^ flip) for i in range(size)])]
    unnamed x1 -> x0, local copies, waits for them, and re-layouts: 0.61 us -> none
    select_n x0 -> x1, local copies, waits for them, and re-layouts: none -> 0.61 us  [local(): values = jnp.where(lax.axis_index('core') == 0, first, second)]
    pallas_call x1, Pallas kernels: 12.4 us -> 12.9 us  [board_values(): pl.pallas_call(functools.partial(board_kernel, hands=hands), in_specs=[pl...]
    ppermute x4 -> x3, starting transfers between devices: 9.68 us -> 9.61 us  [swaps(): lax.ppermute(values, axis, [(i, i ^ flip) for i in range(size)])]
where the time goes in v5:
time: 45.7 us; the launch traced here: 45.2 us
  starting transfers between devices  16.8 us (37%)
  waiting for transfers between devices  13.5 us (30%)
  Pallas kernels  12.9 us (28%)
  other arithmetic  0.71 us (2%)
  between operations  0.67 us (1%)
  local copies, waits for them, and re-layouts  0.61 us (1%)
    pallas_call x1, Pallas kernels, board_values(): pl.pallas_call(functools.partial(board_kernel, hands=hands), in_specs=[pl...  12.9 us
    ppermute x3, starting transfers between devices, swaps(): lax.ppermute(values, axis, [(i, i ^ flip) for i in range(size)])  9.61 us
    all_to_all x1, waiting for transfers between devices, local(): lax.all_to_all(copies, group, 0, 0).reshape(2, -1, *copies.shape[1:])  7.01 us
    all_to_all x1, starting transfers between devices, local(): lax.all_to_all(copies, group, 0, 0).reshape(2, -1, *copies.shape[1:])  5.95 us
    ppermute x3, waiting for transfers between devices, swaps(): lax.ppermute(values, axis, [(i, i ^ flip) for i in range(size)])  4.73 us
    ppermute x1, waiting for transfers between devices, local(): near = lax.ppermute(total, ('x', 'core'), pairs)  1.74 us
    ppermute x1, starting transfers between devices, local(): near = lax.ppermute(total, ('x', 'core'), pairs)  0.92 us
  transfers between devices with their start and end apart: 6, of which 5 were waited for; matrix products, arithmetic and copies ran while one was open for 1% of the time, Pallas kernels for 0%

profile of v5, /device:TPU:6, one launch (start us, length us, event | category | flops | bytes accessed | tf_op | source)
XLA Modules:
  0.0 45.2 jit_solution(7129030363814744432)
XLA Ops:
  0.6 12.9 %boards.1 = f32[16,2,1326]{2,1,0:T(2,128)} custom-call(s32[2,3]{1,0:T(2,128)} %flop_cards_in.1, s32[2]{0:T(128)} %bitcast.11, s32[2,8]{1,0:T(2,128)} %bitcast.10, s32[16,1326]{1,0:T(8,128)} %bitcast.7, f32[2,1326]{1,0:T(2,128)} %flop_reach_in.1, bf16[2,4,1326]{2,1,0:T(4,128)(2,1)} %bitcast.8, f32[4,4,4]{2,1,0:T(4,128)} %bitcast.9, ...), custom_call_target="tpu_custom_call" | custom-call | tf_op jit(solution)/shard_map/boards/pallas_call | solution.py:178
  13.5 5.9 %all-to-all-start = ((f32[16,2,1326]{2,1,0:T(2,128)}), f32[16,2,1326]{2,1,0:T(2,128)S(1)}, u32[]{:S(2)}, u32[]{:S(2)}) async-start(f32[16,2,1326]{2,1,0:T(2,128)} %boards.1), calls=%async_computation | async-start | bytes 360448 | tf_op jit(solution)/shard_map/all_to_all | solution.py:211
  19.5 7.0 %all-to-all-done = f32[16,2,1326]{2,1,0:T(2,128)S(1)} async-done(((f32[16,2,1326]{2,1,0:T(2,128)}), f32[16,2,1326]{2,1,0:T(2,128)S(1)}, u32[]{:S(2)}, u32[]{:S(2)}) %all-to-all-start) | async-done | bytes 169760 | tf_op jit(solution)/shard_map/all_to_all | solution.py:211
  26.5 0.1 slice_reduce_fusion
  26.6 0.9 %collective-permute-start.1 = (f32[2,1326]{1,0:T(2,128)S(1)}, f32[2,1326]{1,0:T(2,128)S(1)}, u32[]{:S(2)}, u32[]{:S(2)}) collective-permute-start(f32[2,1326]{1,0:T(2,128)S(1)} %get-tuple-element.4), channel_id=1, source_target_pairs={{0,16},{8,56},{16,0},{24,40},{32,48},{40,24},{48,32},{56,8},{1,17}... | collective-permute-start | bytes 31832 | tf_op jit(solution)/shard_map/ppermute | solution.py:216
  27.5 1.1 %collective-permute-start = (f32[2,1326]{1,0:T(2,128)S(1)}, f32[2,1326]{1,0:T(2,128)S(1)}, u32[]{:S(2)}, u32[]{:S(2)}) collective-permute-start(f32[2,1326]{1,0:T(2,128)S(1)} %get-tuple-element.4), channel_id=1, source_target_pairs={{0,32},{16,48},{32,0},{48,16},{1,33},{17,49},{33,1},{49,17},{2,34}... | collective-permute-start | bytes 31832 | tf_op jit(solution)/shard_map/ppermute | solution.py:201
  28.6 1.7 %collective-permute-done.1 = f32[2,1326]{1,0:T(2,128)S(1)} collective-permute-done((f32[2,1326]{1,0:T(2,128)S(1)}, f32[2,1326]{1,0:T(2,128)S(1)}, u32[]{:S(2)}, u32[]{:S(2)}) %collective-permute-start.1) | collective-permute-done | bytes 10640 | tf_op jit(solution)/shard_map/ppermute | solution.py:216
  30.4 0.3 collective-permute-start.2
  30.7 2.0 %collective-permute-done = f32[2,1326]{1,0:T(2,128)S(1)} collective-permute-done((f32[2,1326]{1,0:T(2,128)S(1)}, f32[2,1326]{1,0:T(2,128)S(1)}, u32[]{:S(2)}, u32[]{:S(2)}) %collective-permute-start) | collective-permute-done | bytes 10640 | tf_op jit(solution)/shard_map/ppermute | solution.py:201
  32.7 0.0 collective-permute-done.2
  32.7 3.4 %collective-permute-start.3 = (f32[2,1326]{1,0:T(2,128)S(1)}, f32[2,1326]{1,0:T(2,128)S(1)}, u32[]{:S(2)}, u32[]{:S(2)}) collective-permute-start(f32[2,1326]{1,0:T(2,128)S(1)} %add_add_fusion), channel_id=1, source_target_pairs={{0,64},{64,0},{128,192},{192,128},{1,65},{65,1},{129,193},{193,129... | collective-permute-start | bytes 31832 | tf_op jit(solution)/shard_map/ppermute | solution.py:201
  36.1 1.7 %collective-permute-done.3 = f32[2,1326]{1,0:T(2,128)S(1)} collective-permute-done((f32[2,1326]{1,0:T(2,128)S(1)}, f32[2,1326]{1,0:T(2,128)S(1)}, u32[]{:S(2)}, u32[]{:S(2)}) %collective-permute-start.3) | collective-permute-done | bytes 10640 | tf_op jit(solution)/shard_map/ppermute | solution.py:201
  37.8 5.1 %collective-permute-start.4 = (f32[2,1326]{1,0:T(2,128)S(1)}, f32[2,1326]{1,0:T(2,128)S(1)}, u32[]{:S(2)}, u32[]{:S(2)}) collective-permute-start(f32[2,1326]{1,0:T(2,128)S(1)} %add.22), channel_id=1, source_target_pairs={{0,192},{64,128},{128,64},{192,0},{1,193},{65,129},{129,65},{193,1... | collective-permute-start | bytes 31832 | tf_op jit(solution)/shard_map/ppermute | solution.py:201
  42.9 0.6 %select_n.20 = f32[2,1,1326]{2,1,0:T(1,128)} reshape(f32[2,1326]{1,0:T(2,128)S(1)} %get-tuple-element.5) | data formatting | bytes 21216 | tf_op jit(solution)/shard_map/jit(_where)/select_n | solution.py:213
  43.5 1.1 %collective-permute-done.4 = f32[2,1326]{1,0:T(2,128)S(1)} collective-permute-done((f32[2,1326]{1,0:T(2,128)S(1)}, f32[2,1326]{1,0:T(2,128)S(1)}, u32[]{:S(2)}, u32[]{:S(2)}) %collective-permute-start.4) | collective-permute-done | bytes 10640 | tf_op jit(solution)/shard_map/ppermute | solution.py:201
  44.6 0.6 %add_multiply_fusion = f32[2,1326]{1,0:T(2,128)} fusion(f32[2,1326]{1,0:T(2,128)S(1)} %add.22, f32[2,1326]{1,0:T(2,128)S(1)} %collective-permute-done.4), kind=kLoop, calls=%fused_computation.2 | loop fusion | flops 5304 | bytes 31824 | tf_op jit(solution)/shard_map/div | solution.py:220
  (3 shorter events, 0.0 us)
Async XLA Ops:
  13.5 13.0 %all-to-all-start = ((f32[16,2,1326]{2,1,0:T(2,128)}), f32[16,2,1326]{2,1,0:T(2,128)S(1)}, u32[]{:S(2)}, u32[]{:S(2)}) async-start(f32[16,2,1326]{2,1,0:T(2,128)} %boards.1), calls=%async_computation | async-start | bytes 360448 | tf_op jit(solution)/shard_map/all_to_all | solution.py:211
  26.6 3.8 %collective-permute-start.1 = (f32[2,1326]{1,0:T(2,128)S(1)}, f32[2,1326]{1,0:T(2,128)S(1)}, u32[]{:S(2)}, u32[]{:S(2)}) collective-permute-start(f32[2,1326]{1,0:T(2,128)S(1)} %get-tuple-element.4), channel_id=1, source_target_pairs={{0,16},{8,56},{16,0},{24,40},{32,48},{40,24},{48,32},{56,8},{1,17}... | collective-permute-start | bytes 31832 | tf_op jit(solution)/shard_map/ppermute | solution.py:216
  27.5 5.2 %collective-permute-start = (f32[2,1326]{1,0:T(2,128)S(1)}, f32[2,1326]{1,0:T(2,128)S(1)}, u32[]{:S(2)}, u32[]{:S(2)}) collective-permute-start(f32[2,1326]{1,0:T(2,128)S(1)} %get-tuple-element.4), channel_id=1, source_target_pairs={{0,32},{16,48},{32,0},{48,16},{1,33},{17,49},{33,1},{49,17},{2,34}... | collective-permute-start | bytes 31832 | tf_op jit(solution)/shard_map/ppermute | solution.py:201
  30.4 2.3 %collective-permute-start.2 = (f32[2,1326]{1,0:T(2,128)S(1)}, f32[2,1326]{1,0:T(2,128)S(1)}, u32[]{:S(2)}, u32[]{:S(2)}) collective-permute-start(f32[2,1326]{1,0:T(2,128)S(1)} %collective-permute-done.1), channel_id=1, source_target_pairs={{0,8},{8,0},{1,9},{9,1},{2,10},{10,2},{3,11},{11,3},{4,12},{12,4},... | collective-permute-start | bytes 31832 | tf_op jit(solution)/shard_map/ppermute | solution.py:217
  32.7 5.0 %collective-permute-start.3 = (f32[2,1326]{1,0:T(2,128)S(1)}, f32[2,1326]{1,0:T(2,128)S(1)}, u32[]{:S(2)}, u32[]{:S(2)}) collective-permute-start(f32[2,1326]{1,0:T(2,128)S(1)} %add_add_fusion), channel_id=1, source_target_pairs={{0,64},{64,0},{128,192},{192,128},{1,65},{65,1},{129,193},{193,129... | collective-permute-start | bytes 31832 | tf_op jit(solution)/shard_map/ppermute | solution.py:201
  37.8 6.8 %collective-permute-start.4 = (f32[2,1326]{1,0:T(2,128)S(1)}, f32[2,1326]{1,0:T(2,128)S(1)}, u32[]{:S(2)}, u32[]{:S(2)}) collective-permute-start(f32[2,1326]{1,0:T(2,128)S(1)} %add.22), channel_id=1, source_target_pairs={{0,192},{64,128},{128,64},{192,0},{1,193},{65,129},{129,65},{193,1... | collective-permute-start | bytes 31832 | tf_op jit(solution)/shard_map/ppermute | solution.py:201
